TPU v7x, 256 devices: a whole 4x4x8 slice. The times are simulated.
256 devices in a mesh: dp: 8 (over z), tensor: 32 (over x, y, core).
Axes of the slice: x: 4, y: 4, z: 8, core: 2. Of those that a mesh axis runs over, the one named last changes fastest.
Arguments:
- grad: bfloat16 [8, 8192, 14336], P('dp', 'tensor'), may hold values from -20 to 20
- left_basis: bfloat16 [8192, 256], P('tensor'), may hold values from -0.0625 to 0.0625
- right_basis: bfloat16 [14336, 256], P('dp'), may hold values from -0.046875 to 0.046875
- left_stat: float32 [256, 256], replicated, may hold values from -1 to 30, as said below
- right_stat: float32 [256, 256], replicated, may hold values from -1 to 30, as said below
Outputs:
- update: bfloat16 [8192, 14336], P('tensor', 'dp')
- new_left: float32 [256, 256], replicated
- new_right: float32 [256, 256], replicated
Inputs may be any that keep to these rules, and one draw needn't show every extreme that they name: `left_stat`: symmetric positive definite. `right_stat`: symmetric positive definite.
All inputs are finite; a program needn't handle non-finite values.
Results may differ from a plain program's by a relative error of at most 0.0014.
Values may be sent and summed in bfloat16 or wider, within the bound.
No kernel may reach another device: no remote copies, remote signals or barrier semaphores. Data moves between devices by JAX's collectives and lax.ppermute only.
A program may use at most 128 MiB of HBM per device.

v0:
```python
import jax
import jax.numpy as jnp
from jax import lax
from jax.sharding import PartitionSpec as P

ITERS = 6


HIGH = lax.Precision.HIGHEST


def matmul(a, b):
    return jnp.dot(a, b, precision=HIGH, preferred_element_type=jnp.float32)


def shrink(raw, rank):
    eye = jnp.eye(rank, dtype=jnp.float32)
    return 0.9 * raw + 0.1 * jnp.trace(raw) / rank * eye


def inv_root(stat, rank):
    eye = jnp.eye(rank, dtype=jnp.float32)
    scale = jnp.sqrt(jnp.sum(stat * stat))
    current = eye * scale ** (-0.25)
    moving = stat / scale
    for step in range(ITERS):
        factor = (5.0 * eye - moving) * 0.25
        current = matmul(current, factor)
        square = matmul(factor, factor)
        moving = matmul(square, matmul(square, moving))
    return current


def local(grad, left_basis, right_basis, left_stat, right_stat):
    gradient = grad[0]
    rows, width = gradient.shape
    rank = left_basis.shape[1]
    replicas = lax.axis_size("dp")
    groups = lax.axis_size("tensor")
    contract = (((0,), (0,)), ((), ()))
    columns = gradient
    proj = jnp.dot(
        columns,
        lax.all_gather(right_basis, "dp", axis=0, tiled=True),
        preferred_element_type=jnp.float32,
    )
    left_f = left_basis.astype(jnp.float32)
    right_part = matmul(proj.T, proj)
    cross_part = matmul(left_f.T, proj)
    columns = gradient
    coef = lax.psum_scatter(
        lax.dot_general(columns, left_basis, contract, preferred_element_type=jnp.float32),
        "tensor",
        scatter_dimension=0,
        tiled=True,
    )
    left_part = matmul(coef.T, coef)
    right_gram, cross = lax.psum((right_part, cross_part), ("dp", "tensor"))
    left_gram = lax.psum(left_part, ("dp", "tensor"))
    cross = cross / replicas
    raw_left = 0.5 * left_stat + 2.0 / (replicas * width) * left_gram
    raw_right = 0.5 * right_stat + 2.0 / (replicas * rows * groups) * right_gram
    new_left = shrink(raw_left, rank)
    new_right = shrink(raw_right, rank)
    root_left = inv_root(new_left, rank)
    root_right = inv_root(new_right, rank)
    middle = matmul(matmul(root_left, cross), root_right)
    factor = (rows * groups * width) ** 0.5 / rank
    update = matmul(matmul(left_f, middle), right_basis.astype(jnp.float32).T) * factor
    return (update.astype(jnp.bfloat16), new_left, new_right)


def solution(mesh):
    in_specs = (P("dp", "tensor", None), P("tensor", None), P("dp", None), P(), P())
    out_specs = (P("tensor", "dp"), P(), P())
    return jax.shard_map(local, mesh=mesh, in_specs=in_specs, out_specs=out_specs, check_vma=False)
```

profile of v0, /device:TPU:1, one launch (start us, length us, event | category | flops | bytes accessed | tf_op | source)
XLA Modules:
  0.0 432.7 jit_solution(4317072764022183823)
XLA Ops:
  8.1 0.7 all-gather.2.cloned.1.call-update
  8.9 10.4 %fusion.2 = f32[14336,256]{1,0:T(8,128)} fusion(bf16[256,256]{1,0:T(8,128)(2,1)S(1)} %copy-done, bf16[1,256,14336]{2,1,0:T(8,128)(2,1)} %param.5), kind=kOutput, calls=%fused_computation.2 | convolution fusion | flops 1879048192 | bytes 22151168 | tf_op jit(solution)/shard_map/dot_general | solution.py:52
  19.6 79.2 %all-gather.2.cloned.1.call-done = bf16[14336,256]{1,0:T(8,128)(2,1)} async-done(((bf16[1792,256]{1,0:T(8,128)(2,1)}), bf16[14336,256]{1,0:T(8,128)(2,1)}) %all-gather.2.cloned.1.call-update) | async-done | bytes 7340048 | tf_op jit(solution)/shard_map/all_gather | solution.py:44
  98.8 7.5 %fusion = f32[256,256]{1,0:T(8,128)S(1)} fusion(bf16[14336,256]{1,0:T(8,128)(2,1)} %all-gather.2.cloned.1.call-done, bf16[1,256,14336]{2,1,0:T(8,128)(2,1)} %param.5), kind=kOutput, calls=%fused_computation | convolution fusion | flops 1879048192 | bytes 14942208 | tf_op jit(solution)/shard_map/dot_general | solution.py:42
  106.3 1.1 convolution_bitcast_fusion
  107.4 1.3 fusion.197
  108.7 30.8 %reduce-scatter.2.cloned.1.call-done = f32[448,256]{1,0:T(8,128)} async-done(((f32[14336,256]{1,0:T(8,128)}), f32[448,256]{1,0:T(8,128)}) %reduce-scatter.2.cloned.1.call-update) | async-done | bytes 458768 | tf_op jit(solution)/shard_map/reduce_scatter | solution.py:51
  139.6 2.9 fusion.187
  142.5 254.0 %all-reduce.3.cloned.1.call-done = (f32[256,256]{1,0:T(8,128)}, f32[256,256]{0,1:T(8,128)}, f32[256,256]{1,0:T(8,128)}) async-done(((f32[256,256]{1,0:T(8,128)}, f32[256,256]{0,1:T(8,128)}, f32[256,256]{1,0:T(8,128)}), (f32[256,256]{1,0:T(8,128)}, f32[256,256]{0,1:T(8,128)}, f32[256,256]{1,0:T(8,128)})) %all-reduce.3.cloned.1.call-update) | async-done | bytes 786448 | tf_op jit(solution)/shard_map/psum | solution.py:59
  396.5 1.6 select_reduce_fusion
  398.8 1.6 select_reduce_fusion.1
  401.0 1.8 multiply_reduce_fusion
  403.5 0.4 fusion.58
  403.9 0.4 fusion.21
  405.2 0.4 fusion.54
  405.6 0.4 fusion.56
  406.8 0.4 fusion.50
  407.2 0.4 fusion.52
  408.4 0.4 fusion.46
  408.8 0.4 fusion.48
  410.0 0.4 fusion.42
  410.4 0.4 fusion.44
  412.3 0.4 fusion.39
  412.8 0.7 fusion.17
  414.2 0.4 fusion.35
  414.7 0.4 fusion.37
  415.8 0.4 fusion.31
  416.3 0.4 fusion.33
  417.9 0.4 fusion.29
  419.5 0.4 fusion.25
  421.0 0.4 fusion.19
  422.6 2.6 fusion.4
  (45 shorter events, 10.4 us)
Async XLA Ops:
  8.0 0.9 copy-start
  8.0 90.8 %all-gather.2.cloned.1.call-start = ((), (), s32[]{:S(2)}) async-start(), calls=%async_computation.2 | async-start | bytes 8257536 | tf_op jit(solution)/shard_map/all_gather | solution.py:44
  8.7 130.8 %reduce-scatter.2.cloned.1.call-start = ((), (), s32[]{:S(2)}) async-start(), calls=%async_computation.1 | async-start | bytes 15138816 | tf_op jit(solution)/shard_map/reduce_scatter | solution.py:51
  19.4 377.1 %copy-start.2 = (f32[256,256]{1,0:T(8,128)S(1)}, f32[256,256]{1,0:T(8,128)}, u32[]{:S(2)}) copy-start(f32[256,256]{1,0:T(8,128)} %param.9) | copy-start | bytes 786436
  19.4 379.4 %copy-start.3 = (f32[256,256]{1,0:T(8,128)S(1)}, f32[256,256]{1,0:T(8,128)}, u32[]{:S(2)}) copy-start(f32[256,256]{1,0:T(8,128)} %param.8) | copy-start | bytes 786436
  19.4 377.1 %all-reduce.3.cloned.1.call-start = ((), (), s32[]{:S(2)}) async-start(), calls=%async_computation.3 | async-start | bytes 1572864 | tf_op jit(solution)/shard_map/psum | solution.py:59
  402.8 8.4 %copy-start.6 = (f32[256,256]{1,0:T(8,128)}, f32[256,256]{1,0:T(8,128)S(1)}, u32[]{:S(2)}) copy-start(f32[256,256]{1,0:T(8,128)S(1)} %get-tuple-element.11) | copy-start | bytes 786436
  402.8 10.6 %copy-start.5 = (f32[256,256]{1,0:T(8,128)}, f32[256,256]{1,0:T(8,128)S(1)}, u32[]{:S(2)}) copy-start(f32[256,256]{1,0:T(8,128)S(1)} %get-tuple-element.7) | copy-start | bytes 786436
  413.4 7.6 %copy-start.4 = (f32[256,256]{0,1:T(8,128)S(1)}, f32[256,256]{0,1:T(8,128)}, u32[]{:S(2)}) copy-start(f32[256,256]{0,1:T(8,128)} %get-tuple-element.4) | copy-start | bytes 786436
  414.6 8.0 %copy-start.1 = (bf16[1792,256]{1,0:T(8,128)(2,1)S(1)}, bf16[1792,256]{1,0:T(8,128)(2,1)}, u32[]{:S(2)}) copy-start(bf16[1792,256]{1,0:T(8,128)(2,1)} %param.7) | copy-start | bytes 2752516
Sparse Core Ops, SparseCore 0:
  10.6 88.1 all-gather.1
  142.6 253.8 all-reduce.2
Sparse Core Ops, SparseCore 1:
  19.4 120.1 reduce-scatter.1
where the time goes:
time: 433 us
  waiting for transfers between devices  365 us (84%)
  matrix products  43.8 us (10%)
  between operations  18.7 us (4%)
  other arithmetic  4.98 us (1%)
    psum x1, waiting for transfers between devices, local(): left_gram = lax.psum(left_part, ('dp', 'tensor'))  254 us
    all_gather x1, waiting for transfers between devices, local(): lax.all_gather(right_basis, 'dp', axis=0, tiled=True)  79.2 us
    reduce_scatter x1, waiting for transfers between devices, local(): lax.psum_scatter(lax.dot_general(columns, left_basis, contract, preferred...  30.8 us
    dot_general x49, matrix products, matmul(): return jnp.dot(a, b, precision=HIGH, preferred_element_type=jnp.float32)  25.8 us
    dot_general x1, matrix products, local(): lax.dot_general(columns, left_basis, contract, preferred_element_type=jnp...  10.4 us
  transfers between devices with their start and end apart: 3, of which 3 were waited for; matrix products, arithmetic and copies ran while one was open for 5% of the time, Pallas kernels for 0%

commit v1 on v0

v1 whole, which is shorter than its diff:
```python
import functools

import jax
import jax.numpy as jnp
from jax import lax
from jax.experimental import pallas as pl
from jax.experimental.pallas import tpu as pltpu
from jax.sharding import Mesh
from jax.sharding import PartitionSpec as P

ITERS = 6
NX = 4
NY = 4
NZ = 8
ORDER = ((2, 0), (1, 1), (2, 1), (3, 0), (1, 0), (3, 1), (0, 0), (0, 1))
EARLY = 4
F32 = jnp.float32
BF16 = jnp.bfloat16
TRANS = (((0,), (0,)), ((), ()))
PLAIN = (((1,), (0,)), ((), ()))


def dot(a, b, dims=PLAIN):
    return lax.dot_general(a, b, dims, preferred_element_type=F32)


def split(a):
    high = a.astype(BF16)
    return high, (a - high.astype(F32)).astype(BF16)


def mul(a, b, dims=PLAIN):
    return dot(a[0], b[0], dims) + (dot(a[0], b[1], dims) + dot(a[1], b[0], dims))


def params(mib):
    return pltpu.CompilerParams(vmem_limit_bytes=mib * 1024 * 1024)


def shift(x, step):
    pairs = []
    for px in range(NX):
        for py in range(NY):
            pairs.append(((px * NY + py) * 2, (((px + step) % NX) * NY + py) * 2))
            pairs.append(((px * NY + py) * 2 + 1, (px * NY + (py + step) % NY) * 2 + 1))
    return lax.ppermute(x, ("x", "y", "c"), pairs)


def shift_other(x, step):
    pairs = []
    for px in range(NX):
        for py in range(NY):
            pairs.append(((px * NY + py) * 2, (px * NY + (py + step) % NY) * 2))
            pairs.append(((px * NY + py) * 2 + 1, (((px + step) % NX) * NY + py) * 2 + 1))
    return lax.ppermute(x, ("x", "y", "c"), pairs)


def ring(x, step):
    return lax.ppermute(x, "z", [(i, (i + step) % NZ) for i in range(NZ)])


def tie(*arrays):
    return lax.optimization_barrier(arrays)


def swap(x):
    return lax.ppermute(x, "c", [(0, 1), (1, 0)])


def everyone(x, axes, size):
    return lax.all_to_all(jnp.broadcast_to(x[None], (size,) + x.shape), axes, 0, 0)


def place(block, first, per):
    owner = lax.rem(block // per - first + NX, NX)
    half = lax.rem(block, per)
    spot = jnp.int32(ORDER.index((0, 0)))
    for i, (who, which) in enumerate(ORDER):
        spot = jnp.where((owner == who) & (half == which), i, spot)
    return spot


def source(i, first, per):
    who, which = ORDER[i]
    return lax.rem(first + who, NX) * per + which


def cost(flops, moved):
    return pl.CostEstimate(flops=flops, bytes_accessed=moved, transcendentals=0)


def deal_kernel(wide, plans, where, grad, *rest):
    outs, sems = rest[:-1], rest[-1]
    core = where[0]
    copies = []
    for (own, low, high), out in zip(plans, outs):
        first = where[1] if own else where[2]
        half = core if own else 1 - core
        for i in range(low, high):
            column = pl.multiple_of((2 * source(i, first, 2) + half) * wide, 128)
            item = pltpu.make_async_copy(
                grad.at[:, pl.ds(column, wide)], out.at[:, pl.ds((i - low) * wide, wide)], sems.at[len(copies)]
            )
            item.start()
            copies.append(item)
    for item in copies:
        item.wait()


def deal(where, grad, wide, plans):
    rows = grad.shape[0]
    count = sum(high - low for _, low, high in plans)
    vmem = pl.BlockSpec(memory_space=pltpu.VMEM)
    return pl.pallas_call(
        functools.partial(deal_kernel, wide, plans),
        out_shape=tuple(jax.ShapeDtypeStruct((rows, (high - low) * wide), grad.dtype) for _, low, high in plans),
        in_specs=[pl.BlockSpec(memory_space=pltpu.SMEM), pl.BlockSpec(memory_space=pl.ANY)],
        out_specs=tuple(vmem for _ in plans),
        scratch_shapes=[pltpu.SemaphoreType.DMA((count,))],
        compiler_params=params(10),
        name="deal",
    )(where, grad)


def coef_kernel(wide, offset, keep, got, left, left_got, *outs):
    at = 0
    for out in outs:
        for row in range(0, out.shape[0], wide):
            here = pl.ds((offset + at) * wide, wide)
            there = pl.ds(at * wide, wide)
            value = dot(keep[:, here], left[...], TRANS) + dot(got[:, there], left_got[...], TRANS)
            out[row : row + wide, :] = value.astype(out.dtype)
            at += 1


def coef_call(keep, got, left, left_got, wide, offset, counts):
    rank = left.shape[1]
    vmem = pl.BlockSpec(memory_space=pltpu.VMEM)
    return pl.pallas_call(
        functools.partial(coef_kernel, wide, offset),
        out_shape=tuple(jax.ShapeDtypeStruct((n * wide, rank), BF16) for n in counts),
        in_specs=[vmem] * 4,
        out_specs=tuple(vmem for _ in counts),
        compiler_params=params(12),
        name="coef",
    )(keep, got, left, left_got)


def proj_kernel(wide, steps, where, keep, got_early, got_late, *rest):
    blocks, rest = rest[: len(steps)], rest[len(steps) :]
    mine, theirs = rest[-2:]
    if len(rest) == 4:
        mine[...] = rest[0][...]
        theirs[...] = rest[1][...]
    else:
        mine[...] = jnp.zeros_like(mine)
        theirs[...] = jnp.zeros_like(theirs)
    first, replica = where[1], where[3]
    for (step, skip), block in zip(steps, blocks):
        spot = place(lax.rem(replica + step + NZ, NZ), first, 2)
        size = block.shape[0]

        def columns(at):
            return pl.ds(pl.multiple_of(at * wide + skip, 128), size)

        mine[...] += dot(keep[:, columns(spot)], block[...])

        @pl.when(spot < EARLY)
        def _():
            theirs[...] += dot(got_early[:, columns(spot)], block[...])

        @pl.when(spot >= EARLY)
        def _():
            theirs[...] += dot(got_late[:, columns(spot - EARLY)], block[...])


def proj_call(where, keep, got_early, got_late, blocks, steps, wide, sums=()):
    rows = keep.shape[0]
    rank = blocks[0].shape[1]
    shape = jax.ShapeDtypeStruct((rows, rank), F32)
    vmem = pl.BlockSpec(memory_space=pltpu.VMEM)
    return pl.pallas_call(
        functools.partial(proj_kernel, wide, steps),
        out_shape=(shape, shape),
        in_specs=[pl.BlockSpec(memory_space=pltpu.SMEM)] + [vmem] * (3 + len(blocks) + len(sums)),
        out_specs=(vmem, vmem),
        compiler_params=params(12),
        name="proj",
    )(where, keep, got_early, got_late, *blocks, *sums)


def left_gram_kernel(c0, c1, c2, c3, out):
    coef = split(
        (c0[...].astype(F32) + c1[...].astype(F32)) + (c2[...].astype(F32) + c3[...].astype(F32))
    )
    out[...] = mul(coef, coef, TRANS)


def left_gram_call(terms):
    rank = terms[0].shape[1]
    vmem = pl.BlockSpec(memory_space=pltpu.VMEM)
    return pl.pallas_call(
        left_gram_kernel,
        out_shape=jax.ShapeDtypeStruct((rank, rank), F32),
        in_specs=[vmem] * 4,
        out_specs=vmem,
        compiler_params=params(12),
        cost_estimate=cost(6 * rank**3, 16 * rank**2),
        name="left_gram",
    )(*terms)


def gram_kernel(where, mine, theirs, left, left_part, keep, send, parts):
    rank = left.shape[1]
    half = rank // 2
    proj = split(mine[...] + theirs[...])
    basis = left[...]
    parts[:, 0:rank] = left_part[...]
    parts[:, rank : 2 * rank] = mul(proj, proj, TRANS)
    parts[:, 2 * rank :] = dot(basis, proj[0], TRANS) + dot(basis, proj[1], TRANS)
    core = where[0]
    keep[...] = parts[pl.ds(pl.multiple_of(core * half, half), half), :]
    send[...] = parts[pl.ds(pl.multiple_of((1 - core) * half, half), half), :]


def gram_call(where, mine, theirs, left, left_part):
    rank = left.shape[1]
    shape = jax.ShapeDtypeStruct((rank // 2, 3 * rank), F32)
    vmem = pl.BlockSpec(memory_space=pltpu.VMEM)
    return pl.pallas_call(
        gram_kernel,
        out_shape=(shape, shape),
        in_specs=[pl.BlockSpec(memory_space=pltpu.SMEM)] + [vmem] * 4,
        out_specs=(vmem, vmem),
        scratch_shapes=[pltpu.VMEM((rank, 3 * rank), F32)],
        compiler_params=params(12),
        cost_estimate=cost(10 * rank**3, 24 * rank**2),
        name="grams",
    )(where, mine, theirs, left, left_part)


def unit(rank):
    rows = lax.broadcasted_iota(jnp.int32, (rank, rank), 0)
    cols = lax.broadcasted_iota(jnp.int32, (rank, rank), 1)
    return (rows == cols).astype(F32)


def total(a):
    return jnp.sum(jnp.sum(a, axis=1, keepdims=True), axis=0, keepdims=True)


def roots(stats, eye):
    scales = [jnp.sqrt(total(s * s)) for s in stats]
    currents = [None] * len(stats)
    movings = [s / c for s, c in zip(stats, scales)]
    for step in range(ITERS):
        factors = [(5.0 * eye - m) * 0.25 for m in movings]
        parts = [split(f) for f in factors]
        if step == 0:
            currents = [f * lax.rsqrt(jnp.sqrt(c)) for f, c in zip(factors, scales)]
        else:
            currents = [mul(f, split(x)) for x, f in zip(currents, parts)]
        if step < ITERS - 1:
            squares = [split(mul(f, f)) for f in parts]
            firsts = [split(mul(s, split(m))) for s, m in zip(squares, movings)]
            movings = [mul(s, f) for s, f in zip(squares, firsts)]
    return currents


def final_kernel(scales, where, mine, theirs, left_stat, right_stat, left, right, update, new_left, new_right, sums):
    rank = left.shape[1]
    half = rank // 2
    core = where[0]
    sums[pl.ds(pl.multiple_of(core * half, half), half), :] = mine[...]
    sums[pl.ds(pl.multiple_of((1 - core) * half, half), half), :] = theirs[...]
    eye = unit(rank)
    news = []
    for i, stat in enumerate((left_stat, right_stat)):
        raw = 0.5 * stat[...] + scales[i] * sums[:, i * rank : (i + 1) * rank]
        news.append(0.9 * raw + (0.1 / rank) * total(raw * eye) * eye)
    new_left[...] = news[0]
    new_right[...] = news[1]
    root_left, root_right = roots(news, eye)
    cross = sums[:, 2 * rank :] * scales[2]
    middle = mul(split(mul(split(root_left), split(cross))), split(root_right))
    middle = split(middle * scales[3])
    basis = left[...]
    rotated = split(dot(basis, middle[0]) + dot(basis, middle[1]))
    other = right[...]
    dims = (((1,), (1,)), ((), ()))
    update[...] = (dot(rotated[0], other, dims) + dot(rotated[1], other, dims)).astype(update.dtype)


def final_call(scales, where, mine, theirs, left_stat, right_stat, left, right):
    rank = left.shape[1]
    vmem = pl.BlockSpec(memory_space=pltpu.VMEM)
    small = jax.ShapeDtypeStruct((rank, rank), F32)
    return pl.pallas_call(
        functools.partial(final_kernel, scales),
        out_shape=(jax.ShapeDtypeStruct((left.shape[0], right.shape[0]), BF16), small, small),
        in_specs=[pl.BlockSpec(memory_space=pltpu.SMEM)] + [vmem] * 6,
        out_specs=(vmem, vmem, vmem),
        scratch_shapes=[pltpu.VMEM((rank, 3 * rank), F32)],
        compiler_params=params(12),
        name="roots_and_update",
    )(where, mine, theirs, left_stat, right_stat, left, right)


def local(grad, left_basis, right_basis, left_stat, right_stat):
    gradient = grad[0]
    rows, width = gradient.shape
    rank = left_basis.shape[1]
    replicas = lax.axis_size("z")
    groups = lax.axis_size(("x", "y", "c"))
    core = lax.axis_index("c")
    px, py = lax.axis_index("x"), lax.axis_index("y")
    first = jnp.where(core == 0, px, py)
    second = jnp.where(core == 0, py, px)
    first_other = jnp.where(core == 0, py, px)
    where = jnp.stack([core, first, first_other, lax.axis_index("z")]).astype(jnp.int32)

    wide = width // (2 * replicas)

    def proj(blocks, steps, sums=()):
        return proj_call(where, keep, got_early, got_late, blocks, steps, wide, sums)

    own = lax.dynamic_index_in_dim(right_basis.reshape(2, wide, rank), core, 0, keepdims=False)
    gradient, own = tie(gradient, own)
    up1, down1 = ring(own, 1), ring(own, -1)
    (send_early,) = deal(where, gradient, wide, ((False, 0, EARLY),))
    got_early = swap(send_early)
    left_got = swap(left_basis)
    (send_late,) = deal(where, gradient, wide, ((False, EARLY, len(ORDER)),))
    got_late = swap(send_late)
    gradient, left_got = tie(gradient, left_got)
    (keep,) = deal(where, gradient, wide, ((True, 0, len(ORDER)),))

    up, down = coef_call(keep, got_early, left_basis, left_got, wide, 0, (2, 2))
    up1, down1, up, down = tie(up1, down1, up, down)
    up, down = shift(up, 1), shift(down, -1)
    up2, down2 = ring(up1, 1), ring(down1, -1)
    got_late, up1, down1 = tie(got_late, up1, down1)
    up_rest, down_rest, held = coef_call(keep, got_late, left_basis, left_got, wide, EARLY, (1, 1, 2))
    sums = proj([own, up1, down1], ((0, 0), (-1, 0), (1, 0)))
    up2, down2, up_rest, down_rest, *sums = tie(up2, down2, up_rest, down_rest, *sums)

    up3, down3 = ring(up2, 1), ring(down2, -1)
    up, down, up2, down2 = tie(up, down, up2, down2)
    up_rest = shift(up_rest + up[:wide], 1)
    down_rest = shift(down_rest + down[:wide], -1)
    sums = proj([up2, down2], ((-2, 0), (2, 0)), sums)
    up3, down3, *sums = tie(up3, down3, *sums)

    cut = (wide // 2 + 127) // 128 * 128
    far_low, far_high = ring(up3[:cut], 1), ring(down3[cut:], -1)
    up_rest, down_rest, up3, down3 = tie(up_rest, down_rest, up3, down3)
    low = held[:wide].astype(F32) + down[wide:].astype(F32) + up_rest.astype(F32)
    high = held[wide:].astype(F32) + up[wide:].astype(F32) + down_rest.astype(F32)
    held = jnp.concatenate([low, high]).astype(BF16).reshape(NY, -1, rank)

    def owner(k):
        return lax.dynamic_index_in_dim(held, lax.rem(second + k, NY), 0, keepdims=False)

    terms = [owner(0)] + [shift_other(owner(k), k) for k in range(1, NY)]
    sums = proj([up3, down3], ((-3, 0), (3, 0)), sums)
    far_low, far_high, *sums = tie(far_low, far_high, *sums)
    *terms, far_low, far_high = tie(*terms, far_low, far_high)
    left_part = left_gram_call(terms)
    mine, theirs = proj([far_low, far_high], ((NZ // 2, 0), (NZ // 2, cut)), sums)
    stay, send = gram_call(where, mine, swap(theirs), left_basis, left_part)
    plane = NX * NY
    halves = (stay + swap(send)).reshape(plane, -1, 3 * rank)
    rows_sum = jnp.sum(lax.all_to_all(halves, ("x", "y"), 0, 0), axis=0)
    rows_sum = jnp.sum(everyone(rows_sum, "z", replicas), axis=0)
    sums = everyone(rows_sum, ("x", "y"), plane).reshape(-1, 3 * rank)
    scales = (
        2.0 / (replicas * width),
        2.0 / (replicas * rows * groups),
        1.0 / replicas,
        (rows * groups * width) ** 0.5 / rank,
    )
    return final_call(scales, where, sums, swap(sums), left_stat, right_stat, left_basis, right_basis)


def solution(mesh):
    tensor = ("x", "y", "c")
    fine = Mesh(mesh.devices.reshape(mesh.shape["dp"], NX, NY, 2), ("z",) + tensor)
    in_specs = (P("z", tensor, None), P(tensor, None), P("z", None), P(), P())
    out_specs = (P(tensor, "z"), P(), P())
    return jax.shard_map(local, mesh=fine, in_specs=in_specs, out_specs=out_specs, check_vma=False)
```

time: 433 us -> 131 us (0.30)
  waiting for transfers between devices: 365 us -> 21.2 us
  matrix products: 43.8 us -> 0 us
  blocking collectives: 0 us -> 37 us
  starting transfers between devices: 0.3 us -> 34.4 us
  Pallas kernels: 0 us -> 23.2 us
  between operations: 18.7 us -> 1 us
  local copies, waits for them, and re-layouts: 0.15 us -> 9.85 us
    psum x1 -> x0, waiting for transfers between devices: 254 us -> none  [local(): left_gram = lax.psum(left_part, ('dp', 'tensor'))]
    all_gather x1 -> x0, waiting for transfers between devices: 79.2 us -> none  [local(): lax.all_gather(right_basis, 'dp', axis=0, tiled=True)]
    dot_general x51 -> x0, matrix products: 43.8 us -> none  [the longest x49 25.8 us: matmul(): return jnp.dot(a, b, precision=HIGH, preferred_element_type=jnp.float32)]
    all_to_all x0 -> x3, blocking collectives: none -> 37 us  [the longest x2 24.5 us: everyone(): lax.all_to_all(jnp.broadcast_to(x[None], (size,) + x.shape), axes, 0, 0)]
    ppermute x0 -> x21, starting transfers between devices: none -> 34.4 us  [the longest x8 12.1 us: ring(): return lax.ppermute(x, 'z', [(i, (i + step) % NZ) for i in range(NZ)])]
    reduce_scatter x1 -> x0, waiting for transfers between devices: 30.8 us -> none  [local(): lax.psum_scatter(lax.dot_general(columns, left_basis, contract, preferred...]
    pallas_call x0 -> x12, Pallas kernels: none -> 23.2 us  [the longest x1 8.72 us: final_call(): pl.pallas_call(functools.partial(final_kernel, scales), out_shape=(jax.Sh...]
    ppermute x0 -> x21, waiting for transfers between devices: none -> 21.2 us  [the longest x8 14.2 us: ring(): return lax.ppermute(x, 'z', [(i, (i + step) % NZ) for i in range(NZ)])]
  transfers between devices with their start and end apart: 3 -> 21, of which waited for: 3 -> 9; matrix products, arithmetic and copies ran while one was open for 5% -> 3% of each run, Pallas kernels for 0% -> 9%
where the time goes in v1:
time: 131 us; the launch traced here: 130 us
  blocking collectives  37 us (28%)
  starting transfers between devices  34.4 us (26%)
  Pallas kernels  23.2 us (18%)
  waiting for transfers between devices  21.2 us (16%)
  local copies, waits for them, and re-layouts  9.85 us (8%)
  other arithmetic  3.63 us (3%)
    all_to_all x2, blocking collectives, everyone(): lax.all_to_all(jnp.broadcast_to(x[None], (size,) + x.shape), axes, 0, 0)  24.5 us
    ppermute x8, waiting for transfers between devices, ring(): return lax.ppermute(x, 'z', [(i, (i + step) % NZ) for i in range(NZ)])  14.2 us
    all_to_all x1, blocking collectives, local(): rows_sum = jnp.sum(lax.all_to_all(halves, ('x', 'y'), 0, 0), axis=0)  12.5 us
    ppermute x8, starting transfers between devices, ring(): return lax.ppermute(x, 'z', [(i, (i + step) % NZ) for i in range(NZ)])  12.1 us
    ppermute x6, starting transfers between devices, swap(): return lax.ppermute(x, 'c', [(0, 1), (1, 0)])  11.9 us
    pallas_call x1, Pallas kernels, final_call(): pl.pallas_call(functools.partial(final_kernel, scales), out_shape=(jax.Sh...  8.72 us
    unnamed x42, local copies, waits for them, and re-layouts  8.65 us
    pallas_call x4, Pallas kernels, proj_call(): pl.pallas_call(functools.partial(proj_kernel, wide, steps), out_shape=(sh...  7.99 us
  transfers between devices with their start and end apart: 21, of which 9 were waited for; matrix products, arithmetic and copies ran while one was open for 3% of the time, Pallas kernels for 9%

profile of v1, /device:TPU:1, one launch (start us, length us, event | category | flops | bytes accessed | tf_op | source)
XLA Modules:
  0.0 130.3 jit_solution(6895609638780685969)
XLA Ops:
  1.8 3.1 %copy-done.3 = bf16[1,256,14336]{2,1,0:T(8,128)(2,1)S(1)} copy-done((bf16[1,256,14336]{2,1,0:T(8,128)(2,1)S(1)}, bf16[1,256,14336]{2,1,0:T(8,128)(2,1)}, u32[]{:S(2)}) %copy-start.3) | copy-done | bytes 7340056
  5.7 3.3 %collective-permute-start.1 = (bf16[256,3584]{1,0:T(8,128)(2,1)S(1)}, bf16[256,3584]{1,0:T(8,128)(2,1)S(1)}, u32[]{:S(2)}, u32[]{:S(2)}) collective-permute-start(bf16[256,3584]{1,0:T(8,128)(2,1)S(1)} %deal.4), channel_id=1, source_target_pairs={{0,1},{1,0},{2,3},{3,2},{4,5},{5,4},{6,7},{7,6},{8,9},{9,8},{10,11... | collective-permute-start | bytes 5505032 | tf_op jit(solution)/shard_map/ppermute | solution.py:67
  9.9 3.9 %collective-permute-start.4 = (bf16[896,256]{1,0:T(8,128)(2,1)S(1)}, bf16[896,256]{1,0:T(8,128)(2,1)S(1)}, u32[]{:S(2)}, u32[]{:S(2)}) collective-permute-start(bf16[896,256]{1,0:T(8,128)(2,1)S(1)} %dynamic-slice_bitcast_fusion.rest_0_), channel_id=1, source_target_pairs={{0,224},{32,0},{64,32},{96,64},{128,96},{160,128},{192,160},{224,1... | collective-permute-start | bytes 1376264 | tf_op jit(solution)/shard_map/ppermute | solution.py:59
  15.5 1.1 deal.3.keep
  16.7 1.2 coef.2
  17.9 5.4 %collective-permute-done.4.rest_2_ = bf16[896,256]{1,0:T(8,128)(2,1)S(1)} collective-permute-done((bf16[896,256]{1,0:T(8,128)(2,1)S(1)}, bf16[896,256]{1,0:T(8,128)(2,1)S(1)}, u32[]{:S(2)}, u32[]{:S(2)}) %collective-permute-start.4) | collective-permute-done | bytes 458784 | tf_op jit(solution)/shard_map/ppermute | solution.py:59
  23.3 3.1 %collective-permute-done.3.rest_1_ = bf16[896,256]{1,0:T(8,128)(2,1)S(1)} collective-permute-done((bf16[896,256]{1,0:T(8,128)(2,1)S(1)}, bf16[896,256]{1,0:T(8,128)(2,1)S(1)}, u32[]{:S(2)}, u32[]{:S(2)}) %collective-permute-start.3) | collective-permute-done | bytes 458784 | tf_op jit(solution)/shard_map/ppermute | solution.py:59
  26.4 1.3 collective-permute-start.5
  27.7 1.4 %collective-permute-start.6 = (bf16[1792,256]{1,0:T(8,128)(2,1)S(1)}, bf16[1792,256]{1,0:T(8,128)(2,1)S(1)}, u32[]{:S(2)}, u32[]{:S(2)}) collective-permute-start(bf16[1792,256]{1,0:T(8,128)(2,1)S(1)} %get-tuple-element.68), channel_id=1, source_target_pairs={{0,24},{1,7},{2,26},{3,1},{4,28},{5,3},{6,30},{7,5},{8,0},{9,15},{... | collective-permute-start | bytes 2752520 | tf_op jit(solution)/shard_map/ppermute | solution.py:46
  29.1 2.7 %collective-permute-start.8 = (bf16[896,256]{1,0:T(8,128)(2,1)S(1)}, bf16[896,256]{1,0:T(8,128)(2,1)}, u32[]{:S(2)}, u32[]{:S(2)}) collective-permute-start(bf16[896,256]{1,0:T(8,128)(2,1)S(1)} %collective-permute-done.4.rest_2_), channel_id=1, source_target_pairs={{0,224},{32,0},{64,32},{96,64},{128,96},{160,128},{192,160},{224,1... | collective-permute-start | bytes 1376264 | tf_op jit(solution)/shard_map/ppermute | solution.py:59
  31.8 1.2 coef.3
  33.1 2.4 %proj.4 = (f32[256,256]{1,0:T(8,128)S(1)}, f32[256,256]{1,0:T(8,128)S(1)}) custom-call(s32[4]{0:T(128)S(1)} %pad_add_fusion.where, bf16[256,7168]{1,0:T(8,128)(2,1)S(1)} %deal.3.keep, bf16[256,3584]{1,0:T(8,128)(2,1)S(1)} %collective-permute-done.1.got.got_early, bf16[256,3584]{1,0:T(8,128)(2,1)S(1)} %collective-permute-done.2.got.got_late, ...), custom_call_target="tpu_custom_call" | custom-call | tf_op jit(solution)/shard_map/proj/pallas_call | solution.py:182
  35.5 4.8 %collective-permute-done.7.rest_0_ = bf16[896,256]{1,0:T(8,128)(2,1)S(1)} collective-permute-done((bf16[896,256]{1,0:T(8,128)(2,1)S(1)}, bf16[896,256]{1,0:T(8,128)(2,1)S(1)}, u32[]{:S(2)}, u32[]{:S(2)}) %collective-permute-start.7) | collective-permute-done | bytes 458784 | tf_op jit(solution)/shard_map/ppermute | solution.py:59
  40.3 2.7 %collective-permute-start.12 = (bf16[896,256]{1,0:T(8,128)(2,1)}, bf16[896,256]{1,0:T(8,128)(2,1)S(1)}, u32[]{:S(2)}, u32[]{:S(2)}) collective-permute-start(bf16[896,256]{1,0:T(8,128)(2,1)} %collective-permute-done.8.rest_1_), channel_id=1, source_target_pairs={{0,224},{32,0},{64,32},{96,64},{128,96},{160,128},{192,160},{224,1... | collective-permute-start | bytes 1376264 | tf_op jit(solution)/shard_map/ppermute | solution.py:59
  44.7 2.8 %collective-permute-start.10 = (bf16[896,256]{1,0:T(8,128)(2,1)}, bf16[896,256]{1,0:T(8,128)(2,1)}, u32[]{:S(2)}, u32[]{:S(2)}) collective-permute-start(bf16[896,256]{1,0:T(8,128)(2,1)} %slice_add_fusion), channel_id=1, source_target_pairs={{0,24},{1,7},{2,26},{3,1},{4,28},{5,3},{6,30},{7,5},{8,0},{9,15},{... | collective-permute-start | bytes 1376264 | tf_op jit(solution)/shard_map/ppermute | solution.py:46
  47.5 2.0 %copy-done.1 = bf16[256,7168]{1,0:T(8,128)(2,1)S(1)} copy-done((bf16[256,7168]{1,0:T(8,128)(2,1)S(1)}, bf16[256,7168]{1,0:T(8,128)(2,1)}, u32[]{:S(2)}) %copy-start.1) | copy-done | bytes 3670040
  49.5 1.5 %copy-done.5 = bf16[256,3584]{1,0:T(8,128)(2,1)S(1)} copy-done((bf16[256,3584]{1,0:T(8,128)(2,1)S(1)}, bf16[256,3584]{1,0:T(8,128)(2,1)}, u32[]{:S(2)}) %copy-start.5) | copy-done | bytes 1835032
  52.9 2.4 %proj.5 = (f32[256,256]{1,0:T(8,128)S(1)}, f32[256,256]{1,0:T(8,128)S(1)}) custom-call(s32[4]{0:T(128)S(1)} %pad_add_fusion.where, bf16[256,7168]{1,0:T(8,128)(2,1)S(1)} %copy-done.1, bf16[256,3584]{1,0:T(8,128)(2,1)S(1)} %collective-permute-done.1.got.got_early, bf16[256,3584]{1,0:T(8,128)(2,1)S(1)} %copy-done.5, ...), custom_call_target="tpu_custom_call" | custom-call | tf_op jit(solution)/shard_map/proj/pallas_call | solution.py:182
  55.6 1.7 %add_convert_fusion.1 = (bf16[896,256]{1,0:T(8,128)(2,1)S(1)}, bf16[896,256]{1,0:T(8,128)(2,1)S(1)}) fusion(bf16[896,256]{1,0:T(8,128)(2,1)} %collective-permute-done.9, bf16[1792,256]{1,0:T(8,128)(2,1)S(1)} %copy-done.20, bf16[1792,256]{1,0:T(8,128)(2,1)S(1)} %copy-done.10, bf16[896,256]{1,0:T(8,128)(2,1)} %collective-permute-done.10, ...), kind=kLoop, calls=%fused_computation.2 | loop fusion | flops 2752512 | bytes 3670016 | tf_op jit(solution)/shard_map/convert
  57.4 3.8 %collective-permute-start.15 = (bf16[448,256]{1,0:T(8,128)(2,1)S(1)}, bf16[448,256]{1,0:T(8,128)(2,1)S(1)}, u32[]{:S(2)}, u32[]{:S(2)}) collective-permute-start(bf16[448,256]{1,0:T(8,128)(2,1)S(1)} %get-tuple-element.111), channel_id=1, source_target_pairs={{0,6},{1,25},{2,0},{3,27},{4,2},{5,29},{6,4},{7,31},{8,14},{9,1},{... | collective-permute-start | bytes 688136 | tf_op jit(solution)/shard_map/ppermute | solution.py:55
  62.3 2.7 %collective-permute-start.17 = (bf16[384,256]{1,0:T(8,128)(2,1)S(1)}, bf16[384,256]{1,0:T(8,128)(2,1)S(1)}, u32[]{:S(2)}, u32[]{:S(2)}) collective-permute-start(bf16[384,256]{1,0:T(8,128)(2,1)S(1)} %slice.31), channel_id=1, source_target_pairs={{0,224},{32,0},{64,32},{96,64},{128,96},{160,128},{192,160},{224,1... | collective-permute-start | bytes 589832 | tf_op jit(solution)/shard_map/ppermute | solution.py:59
  65.0 1.8 %proj.6 = (f32[256,256]{1,0:T(8,128)S(1)}, f32[256,256]{1,0:T(8,128)S(1)}) custom-call(s32[4]{0:T(128)S(1)} %pad_add_fusion.where, bf16[256,7168]{1,0:T(8,128)(2,1)S(1)} %copy-done.2, bf16[256,3584]{1,0:T(8,128)(2,1)S(1)} %collective-permute-done.1.got.got_early, bf16[256,3584]{1,0:T(8,128)(2,1)S(1)} %copy-done.6, ...), custom_call_target="tpu_custom_call" | custom-call | tf_op jit(solution)/shard_map/proj/pallas_call | solution.py:182
  67.7 2.6 %collective-permute-done.13.c1 = bf16[448,256]{1,0:T(8,128)(2,1)S(1)} collective-permute-done((bf16[448,256]{1,0:T(8,128)(2,1)S(1)}, bf16[448,256]{1,0:T(8,128)(2,1)S(1)}, u32[]{:S(2)}, u32[]{:S(2)}) %collective-permute-start.13) | collective-permute-done | bytes 229408 | tf_op jit(solution)/shard_map/ppermute | solution.py:55
  70.3 1.4 %proj.7 = (f32[256,256]{1,0:T(8,128)S(1)}, f32[256,256]{1,0:T(8,128)S(1)}) custom-call(s32[4]{0:T(128)S(1)} %pad_add_fusion.where, bf16[256,7168]{1,0:T(8,128)(2,1)S(1)} %copy-done.2, bf16[256,3584]{1,0:T(8,128)(2,1)S(1)} %collective-permute-done.1.got.got_early, bf16[256,3584]{1,0:T(8,128)(2,1)S(1)} %copy-done.6, ...), custom_call_target="tpu_custom_call" | custom-call | tf_op jit(solution)/shard_map/proj/pallas_call | solution.py:182
  71.7 3.1 %collective-permute-start.18 = (f32[256,256]{1,0:T(8,128)S(1)}, f32[256,256]{1,0:T(8,128)S(1)}, u32[]{:S(2)}, u32[]{:S(2)}) collective-permute-start(f32[256,256]{1,0:T(8,128)S(1)} %get-tuple-element.104), channel_id=1, source_target_pairs={{0,1},{1,0},{2,3},{3,2},{4,5},{5,4},{6,7},{7,6},{8,9},{9,8},{10,11... | collective-permute-start | bytes 786440 | tf_op jit(solution)/shard_map/ppermute | solution.py:67
  77.4 1.3 %collective-permute-done.19 = f32[128,768]{1,0:T(8,128)S(1)} collective-permute-done((f32[128,768]{1,0:T(8,128)S(1)}, f32[128,768]{1,0:T(8,128)S(1)}, u32[]{:S(2)}, u32[]{:S(2)}) %collective-permute-start.19) | collective-permute-done | bytes 393248 | tf_op jit(solution)/shard_map/ppermute | solution.py:67
  78.9 12.5 %all_to_all.15 = f32[16,8,768]{2,1,0:T(8,128)S(1)} all-to-all(f32[16,8,768]{2,1,0:T(8,128)S(1)} %add_bitcast_fusion), channel_id=1, replica_groups=mesh['z'=8,'x'=4,'y'=4,'c'=2] {'x','y'}, dimensions={0} | all-to-all | bytes 786432 | tf_op jit(solution)/shard_map/all_to_all | solution.py:373
  91.4 13.2 %all_to_all.16 = f32[8,8,768]{2,1,0:T(8,128)S(1)} all-to-all(f32[8,8,768]{2,1,0:T(8,128)S(1)} %broadcast_in_dim.4), channel_id=1, replica_groups=mesh['z'=8,'x'=4,'y'=4,'c'=2] {'z'}, dimensions={0} | all-to-all | bytes 393216 | tf_op jit(solution)/shard_map/all_to_all | solution.py:71
  104.7 11.3 %all_to_all.17 = f32[16,8,768]{2,1,0:T(8,128)S(1)} all-to-all(f32[16,8,768]{2,1,0:T(8,128)S(1)} %broadcast_in_dim.5), channel_id=1, replica_groups=mesh['z'=8,'x'=4,'y'=4,'c'=2] {'x','y'}, dimensions={0} | all-to-all | bytes 786432 | tf_op jit(solution)/shard_map/all_to_all | solution.py:71
  116.0 4.2 %collective-permute-start.20 = (f32[128,768]{1,0:T(8,128)S(1)}, f32[128,768]{1,0:T(8,128)S(1)}, u32[]{:S(2)}, u32[]{:S(2)}) collective-permute-start(f32[128,768]{1,0:T(8,128)S(1)} %bitcast.24), channel_id=1, source_target_pairs={{0,1},{1,0},{2,3},{3,2},{4,5},{5,4},{6,7},{7,6},{8,9},{9,8},{10,11... | collective-permute-start | bytes 1179656 | tf_op jit(solution)/shard_map/ppermute | solution.py:67
  120.2 1.3 %collective-permute-done.20.theirs = f32[128,768]{1,0:T(8,128)S(1)} collective-permute-done((f32[128,768]{1,0:T(8,128)S(1)}, f32[128,768]{1,0:T(8,128)S(1)}, u32[]{:S(2)}, u32[]{:S(2)}) %collective-permute-start.20) | collective-permute-done | bytes 393248 | tf_op jit(solution)/shard_map/ppermute | solution.py:67
  121.6 8.7 %roots_and_update.1 = (bf16[256,1792]{1,0:T(8,128)(2,1)}, f32[256,256]{1,0:T(8,128)}, f32[256,256]{1,0:T(8,128)}) custom-call(s32[4]{0:T(128)S(1)} %pad_add_fusion.where, f32[128,768]{1,0:T(8,128)S(1)} %bitcast.25, f32[128,768]{1,0:T(8,128)S(1)} %collective-permute-done.20.theirs, f32[256,256]{1,0:T(8,128)S(1)} %copy-done.11, f32[256,256]{1,0:T(8,128)S(1)} %copy-done.12, ...), custom_call_target="tpu_custom_call" | custom-call | tf_op jit(solution)/shard_map/roots_and_update/pallas_call | solution.py:298
  (81 shorter events, 13.3 us)
Async XLA Ops:
  1.8 3.1 %copy-start.3 = (bf16[1,256,14336]{2,1,0:T(8,128)(2,1)S(1)}, bf16[1,256,14336]{2,1,0:T(8,128)(2,1)}, u32[]{:S(2)}) copy-start(bf16[1,256,14336]{2,1,0:T(8,128)(2,1)} %param.5) | copy-start | bytes 22020100
  5.7 8.2 %copy-start.7 = (bf16[256,256]{1,0:T(8,128)(2,1)S(1)}, bf16[256,256]{1,0:T(8,128)(2,1)}, u32[]{:S(2)}) copy-start(bf16[256,256]{1,0:T(8,128)(2,1)} %left.7) | copy-start | bytes 393220
  5.7 11.0 %collective-permute-start.1 = (bf16[256,3584]{1,0:T(8,128)(2,1)S(1)}, bf16[256,3584]{1,0:T(8,128)(2,1)S(1)}, u32[]{:S(2)}, u32[]{:S(2)}) collective-permute-start(bf16[256,3584]{1,0:T(8,128)(2,1)S(1)} %deal.4), channel_id=1, source_target_pairs={{0,1},{1,0},{2,3},{3,2},{4,5},{5,4},{6,7},{7,6},{8,9},{9,8},{10,11... | collective-permute-start | bytes 5505032 | tf_op jit(solution)/shard_map/ppermute | solution.py:67
  9.8 22.0 %collective-permute-start.2 = (bf16[256,3584]{1,0:T(8,128)(2,1)S(1)}, bf16[256,3584]{1,0:T(8,128)(2,1)S(1)}, u32[]{:S(2)}, u32[]{:S(2)}) collective-permute-start(bf16[256,3584]{1,0:T(8,128)(2,1)S(1)} %deal.5), channel_id=1, source_target_pairs={{0,1},{1,0},{2,3},{3,2},{4,5},{5,4},{6,7},{7,6},{8,9},{9,8},{10,11... | collective-permute-start | bytes 5505032 | tf_op jit(solution)/shard_map/ppermute | solution.py:67
  9.9 13.4 %collective-permute-start.4 = (bf16[896,256]{1,0:T(8,128)(2,1)S(1)}, bf16[896,256]{1,0:T(8,128)(2,1)S(1)}, u32[]{:S(2)}, u32[]{:S(2)}) collective-permute-start(bf16[896,256]{1,0:T(8,128)(2,1)S(1)} %dynamic-slice_bitcast_fusion.rest_0_), channel_id=1, source_target_pairs={{0,224},{32,0},{64,32},{96,64},{128,96},{160,128},{192,160},{224,1... | collective-permute-start | bytes 1376264 | tf_op jit(solution)/shard_map/ppermute | solution.py:59
  13.8 12.6 %collective-permute-start.3 = (bf16[896,256]{1,0:T(8,128)(2,1)S(1)}, bf16[896,256]{1,0:T(8,128)(2,1)S(1)}, u32[]{:S(2)}, u32[]{:S(2)}) collective-permute-start(bf16[896,256]{1,0:T(8,128)(2,1)S(1)} %dynamic-slice_bitcast_fusion.rest_0_), channel_id=1, source_target_pairs={{0,32},{32,64},{64,96},{96,128},{128,160},{160,192},{192,224},{224... | collective-permute-start | bytes 1376264 | tf_op jit(solution)/shard_map/ppermute | solution.py:59
  13.8 1.7 %collective-permute-start = (bf16[256,256]{1,0:T(8,128)(2,1)S(1)}, bf16[256,256]{1,0:T(8,128)(2,1)S(1)}, u32[]{:S(2)}, u32[]{:S(2)}) collective-permute-start(bf16[256,256]{1,0:T(8,128)(2,1)S(1)} %copy-done.7), channel_id=1, source_target_pairs={{0,1},{1,0},{2,3},{3,2},{4,5},{5,4},{6,7},{7,6},{8,9},{9,8},{10,11... | collective-permute-start | bytes 393224 | tf_op jit(solution)/shard_map/ppermute | solution.py:67
  16.6 16.4 %copy-start = (bf16[256,7168]{1,0:T(8,128)(2,1)}, bf16[256,7168]{1,0:T(8,128)(2,1)S(1)}, u32[]{:S(2)}) copy-start(bf16[256,7168]{1,0:T(8,128)(2,1)S(1)} %deal.3.keep) | copy-start | bytes 11010052
  26.4 16.6 %collective-permute-start.5 = (bf16[1792,256]{1,0:T(8,128)(2,1)S(1)}, bf16[1792,256]{1,0:T(8,128)(2,1)S(1)}, u32[]{:S(2)}, u32[]{:S(2)}) collective-permute-start(bf16[1792,256]{1,0:T(8,128)(2,1)S(1)} %get-tuple-element.67), channel_id=1, source_target_pairs={{0,8},{1,3},{2,10},{3,5},{4,12},{5,7},{6,14},{7,1},{8,16},{9,11},{... | collective-permute-start | bytes 2752520 | tf_op jit(solution)/shard_map/ppermute | solution.py:46
  27.7 15.3 %collective-permute-start.6 = (bf16[1792,256]{1,0:T(8,128)(2,1)S(1)}, bf16[1792,256]{1,0:T(8,128)(2,1)S(1)}, u32[]{:S(2)}, u32[]{:S(2)}) collective-permute-start(bf16[1792,256]{1,0:T(8,128)(2,1)S(1)} %get-tuple-element.68), channel_id=1, source_target_pairs={{0,24},{1,7},{2,26},{3,1},{4,28},{5,3},{6,30},{7,5},{8,0},{9,15},{... | collective-permute-start | bytes 2752520 | tf_op jit(solution)/shard_map/ppermute | solution.py:46
  29.1 11.1 %collective-permute-start.7 = (bf16[896,256]{1,0:T(8,128)(2,1)S(1)}, bf16[896,256]{1,0:T(8,128)(2,1)S(1)}, u32[]{:S(2)}, u32[]{:S(2)}) collective-permute-start(bf16[896,256]{1,0:T(8,128)(2,1)S(1)} %collective-permute-done.3.rest_1_), channel_id=1, source_target_pairs={{0,32},{32,64},{64,96},{96,128},{128,160},{160,192},{192,224},{224... | collective-permute-start | bytes 1376264 | tf_op jit(solution)/shard_map/ppermute | solution.py:59
  29.1 11.1 %collective-permute-start.8 = (bf16[896,256]{1,0:T(8,128)(2,1)S(1)}, bf16[896,256]{1,0:T(8,128)(2,1)}, u32[]{:S(2)}, u32[]{:S(2)}) collective-permute-start(bf16[896,256]{1,0:T(8,128)(2,1)S(1)} %collective-permute-done.4.rest_2_), channel_id=1, source_target_pairs={{0,224},{32,0},{64,32},{96,64},{128,96},{160,128},{192,160},{224,1... | collective-permute-start | bytes 1376264 | tf_op jit(solution)/shard_map/ppermute | solution.py:59
  35.5 9.3 %copy-start.13 = (f32[256,256]{1,0:T(8,128)}, f32[256,256]{1,0:T(8,128)S(1)}, u32[]{:S(2)}) copy-start(f32[256,256]{1,0:T(8,128)S(1)} %get-tuple-element.83.rest_2_) | copy-start | bytes 786436
  35.5 9.3 %copy-start.15 = (f32[256,256]{1,0:T(8,128)}, f32[256,256]{1,0:T(8,128)S(1)}, u32[]{:S(2)}) copy-start(f32[256,256]{1,0:T(8,128)S(1)} %get-tuple-element.84.rest_3_) | copy-start | bytes 786436
  40.3 15.1 %collective-permute-start.11 = (bf16[896,256]{1,0:T(8,128)(2,1)S(1)}, bf16[896,256]{1,0:T(8,128)(2,1)S(1)}, u32[]{:S(2)}, u32[]{:S(2)}) collective-permute-start(bf16[896,256]{1,0:T(8,128)(2,1)S(1)} %collective-permute-done.7.rest_0_), channel_id=1, source_target_pairs={{0,32},{32,64},{64,96},{96,128},{128,160},{160,192},{192,224},{224... | collective-permute-start | bytes 1376264 | tf_op jit(solution)/shard_map/ppermute | solution.py:59
  40.3 15.1 %collective-permute-start.12 = (bf16[896,256]{1,0:T(8,128)(2,1)}, bf16[896,256]{1,0:T(8,128)(2,1)S(1)}, u32[]{:S(2)}, u32[]{:S(2)}) collective-permute-start(bf16[896,256]{1,0:T(8,128)(2,1)} %collective-permute-done.8.rest_1_), channel_id=1, source_target_pairs={{0,224},{32,0},{64,32},{96,64},{128,96},{160,128},{192,160},{224,1... | collective-permute-start | bytes 1376264 | tf_op jit(solution)/shard_map/ppermute | solution.py:59
  43.9 11.6 %collective-permute-start.9 = (bf16[896,256]{1,0:T(8,128)(2,1)}, bf16[896,256]{1,0:T(8,128)(2,1)}, u32[]{:S(2)}, u32[]{:S(2)}) collective-permute-start(bf16[896,256]{1,0:T(8,128)(2,1)} %slice_add_fusion.1), channel_id=1, source_target_pairs={{0,8},{1,3},{2,10},{3,5},{4,12},{5,7},{6,14},{7,1},{8,16},{9,11},{... | collective-permute-start | bytes 1376264 | tf_op jit(solution)/shard_map/ppermute | solution.py:46
  44.7 10.8 %collective-permute-start.10 = (bf16[896,256]{1,0:T(8,128)(2,1)}, bf16[896,256]{1,0:T(8,128)(2,1)}, u32[]{:S(2)}, u32[]{:S(2)}) collective-permute-start(bf16[896,256]{1,0:T(8,128)(2,1)} %slice_add_fusion), channel_id=1, source_target_pairs={{0,24},{1,7},{2,26},{3,1},{4,28},{5,3},{6,30},{7,5},{8,0},{9,15},{... | collective-permute-start | bytes 1376264 | tf_op jit(solution)/shard_map/ppermute | solution.py:46
  52.9 2.6 %copy-start.20 = (bf16[1792,256]{1,0:T(8,128)(2,1)S(1)}, bf16[1792,256]{1,0:T(8,128)(2,1)}, u32[]{:S(2)}) copy-start(bf16[1792,256]{1,0:T(8,128)(2,1)} %copy-done.19) | copy-start | bytes 2752516
  55.4 12.3 %collective-permute-start.16 = (bf16[512,256]{1,0:T(8,128)(2,1)S(1)}, bf16[512,256]{1,0:T(8,128)(2,1)S(1)}, u32[]{:S(2)}, u32[]{:S(2)}) collective-permute-start(bf16[512,256]{1,0:T(8,128)(2,1)S(1)} %slice.30), channel_id=1, source_target_pairs={{0,32},{32,64},{64,96},{96,128},{128,160},{160,192},{192,224},{224... | collective-permute-start | bytes 786440 | tf_op jit(solution)/shard_map/ppermute | solution.py:59
  55.5 9.5 %copy-start.6 = (bf16[256,3584]{1,0:T(8,128)(2,1)S(1)}, bf16[256,3584]{1,0:T(8,128)(2,1)}, u32[]{:S(2)}) copy-start(bf16[256,3584]{1,0:T(8,128)(2,1)} %copy-done.4) | copy-start | bytes 5505028
  57.2 7.8 %copy-start.2 = (bf16[256,7168]{1,0:T(8,128)(2,1)S(1)}, bf16[256,7168]{1,0:T(8,128)(2,1)}, u32[]{:S(2)}) copy-start(bf16[256,7168]{1,0:T(8,128)(2,1)} %copy-done) | copy-start | bytes 11010052
  57.4 10.3 %collective-permute-start.15 = (bf16[448,256]{1,0:T(8,128)(2,1)S(1)}, bf16[448,256]{1,0:T(8,128)(2,1)S(1)}, u32[]{:S(2)}, u32[]{:S(2)}) collective-permute-start(bf16[448,256]{1,0:T(8,128)(2,1)S(1)} %get-tuple-element.111), channel_id=1, source_target_pairs={{0,6},{1,25},{2,0},{3,27},{4,2},{5,29},{6,4},{7,31},{8,14},{9,1},{... | collective-permute-start | bytes 688136 | tf_op jit(solution)/shard_map/ppermute | solution.py:55
  61.2 6.5 %collective-permute-start.14 = (bf16[448,256]{1,0:T(8,128)(2,1)S(1)}, bf16[448,256]{1,0:T(8,128)(2,1)S(1)}, u32[]{:S(2)}, u32[]{:S(2)}) collective-permute-start(bf16[448,256]{1,0:T(8,128)(2,1)S(1)} %get-tuple-element.112), channel_id=1, source_target_pairs={{0,4},{1,17},{2,6},{3,19},{4,0},{5,21},{6,2},{7,23},{8,12},{9,25},... | collective-permute-start | bytes 688136 | tf_op jit(solution)/shard_map/ppermute | solution.py:55
  61.7 8.6 %collective-permute-start.13 = (bf16[448,256]{1,0:T(8,128)(2,1)S(1)}, bf16[448,256]{1,0:T(8,128)(2,1)S(1)}, u32[]{:S(2)}, u32[]{:S(2)}) collective-permute-start(bf16[448,256]{1,0:T(8,128)(2,1)S(1)} %get-tuple-element.113), channel_id=1, source_target_pairs={{0,2},{1,9},{2,4},{3,11},{4,6},{5,13},{6,0},{7,15},{8,10},{9,17},{... | collective-permute-start | bytes 688136 | tf_op jit(solution)/shard_map/ppermute | solution.py:55
  62.3 5.3 %collective-permute-start.17 = (bf16[384,256]{1,0:T(8,128)(2,1)S(1)}, bf16[384,256]{1,0:T(8,128)(2,1)S(1)}, u32[]{:S(2)}, u32[]{:S(2)}) collective-permute-start(bf16[384,256]{1,0:T(8,128)(2,1)S(1)} %slice.31), channel_id=1, source_target_pairs={{0,224},{32,0},{64,32},{96,64},{128,96},{160,128},{192,160},{224,1... | collective-permute-start | bytes 589832 | tf_op jit(solution)/shard_map/ppermute | solution.py:59
  71.7 4.3 %collective-permute-start.18 = (f32[256,256]{1,0:T(8,128)S(1)}, f32[256,256]{1,0:T(8,128)S(1)}, u32[]{:S(2)}, u32[]{:S(2)}) collective-permute-start(f32[256,256]{1,0:T(8,128)S(1)} %get-tuple-element.104), channel_id=1, source_target_pairs={{0,1},{1,0},{2,3},{3,2},{4,5},{5,4},{6,7},{7,6},{8,9},{9,8},{10,11... | collective-permute-start | bytes 786440 | tf_op jit(solution)/shard_map/ppermute | solution.py:67
  77.0 1.8 %collective-permute-start.19 = (f32[128,768]{1,0:T(8,128)S(1)}, f32[128,768]{1,0:T(8,128)S(1)}, u32[]{:S(2)}, u32[]{:S(2)}) collective-permute-start(f32[128,768]{1,0:T(8,128)S(1)} %get-tuple-element.110), channel_id=1, source_target_pairs={{0,1},{1,0},{2,3},{3,2},{4,5},{5,4},{6,7},{7,6},{8,9},{9,8},{10,11... | collective-permute-start | bytes 1179656 | tf_op jit(solution)/shard_map/ppermute | solution.py:67
  78.8 42.7 %copy-start.8 = (bf16[1792,256]{1,0:T(8,128)(2,1)S(1)}, bf16[1792,256]{1,0:T(8,128)(2,1)}, u32[]{:S(2)}) copy-start(bf16[1792,256]{1,0:T(8,128)(2,1)} %right.1) | copy-start | bytes 2752516
  78.9 42.7 %copy-start.11 = (f32[256,256]{1,0:T(8,128)S(1)}, f32[256,256]{1,0:T(8,128)}, u32[]{:S(2)}) copy-start(f32[256,256]{1,0:T(8,128)} %left_stat.1) | copy-start | bytes 786436
  78.9 42.7 %copy-start.12 = (f32[256,256]{1,0:T(8,128)S(1)}, f32[256,256]{1,0:T(8,128)}, u32[]{:S(2)}) copy-start(f32[256,256]{1,0:T(8,128)} %right_stat.1) | copy-start | bytes 786436
  116.0 5.6 %collective-permute-start.20 = (f32[128,768]{1,0:T(8,128)S(1)}, f32[128,768]{1,0:T(8,128)S(1)}, u32[]{:S(2)}, u32[]{:S(2)}) collective-permute-start(f32[128,768]{1,0:T(8,128)S(1)} %bitcast.24), channel_id=1, source_target_pairs={{0,1},{1,0},{2,3},{3,2},{4,5},{5,4},{6,7},{7,6},{8,9},{9,8},{10,11... | collective-permute-start | bytes 1179656 | tf_op jit(solution)/shard_map/ppermute | solution.py:67
  (10 other events, 17.8 us)

commit v2 on v1

--- a/solution.py
+++ b/solution.py
@@ -114,7 +114,7 @@
     return pl.pallas_call(
         functools.partial(deal_kernel, wide, plans),
         out_shape=tuple(jax.ShapeDtypeStruct((rows, (high - low) * wide), grad.dtype) for _, low, high in plans),
-        in_specs=[pl.BlockSpec(memory_space=pltpu.SMEM), pl.BlockSpec(memory_space=pl.ANY)],
+        in_specs=[pl.BlockSpec(memory_space=pltpu.SMEM), pl.BlockSpec(memory_space=pltpu.HBM)],
         out_specs=tuple(vmem for _ in plans),
         scratch_shapes=[pltpu.SemaphoreType.DMA((count,))],
         compiler_params=params(10),
@@ -127,8 +127,7 @@
     for out in outs:
         for row in range(0, out.shape[0], wide):
             here = pl.ds((offset + at) * wide, wide)
-            there = pl.ds(at * wide, wide)
-            value = dot(keep[:, here], left[...], TRANS) + dot(got[:, there], left_got[...], TRANS)
+            value = dot(keep[:, here], left[...], TRANS) + dot(got[:, here], left_got[...], TRANS)
             out[row : row + wide, :] = value.astype(out.dtype)
             at += 1
 
@@ -146,7 +145,7 @@
     )(keep, got, left, left_got)
 
 
-def proj_kernel(wide, steps, where, keep, got_early, got_late, *rest):
+def proj_kernel(wide, steps, where, keep, got, *rest):
     blocks, rest = rest[: len(steps)], rest[len(steps) :]
     mine, theirs = rest[-2:]
     if len(rest) == 4:
@@ -165,16 +164,10 @@
 
         mine[...] += dot(keep[:, columns(spot)], block[...])
 
-        @pl.when(spot < EARLY)
-        def _():
-            theirs[...] += dot(got_early[:, columns(spot)], block[...])
-
-        @pl.when(spot >= EARLY)
-        def _():
-            theirs[...] += dot(got_late[:, columns(spot - EARLY)], block[...])
-
-
-def proj_call(where, keep, got_early, got_late, blocks, steps, wide, sums=()):
+        theirs[...] += dot(got[:, columns(spot)], block[...])
+
+
+def proj_call(where, keep, got, blocks, steps, wide, sums=()):
     rows = keep.shape[0]
     rank = blocks[0].shape[1]
     shape = jax.ShapeDtypeStruct((rows, rank), F32)
@@ -182,11 +175,11 @@
     return pl.pallas_call(
         functools.partial(proj_kernel, wide, steps),
         out_shape=(shape, shape),
-        in_specs=[pl.BlockSpec(memory_space=pltpu.SMEM)] + [vmem] * (3 + len(blocks) + len(sums)),
+        in_specs=[pl.BlockSpec(memory_space=pltpu.SMEM)] + [vmem] * (2 + len(blocks) + len(sums)),
         out_specs=(vmem, vmem),
         compiler_params=params(12),
         name="proj",
-    )(where, keep, got_early, got_late, *blocks, *sums)
+    )(where, keep, got, *blocks, *sums)
 
 
 def left_gram_kernel(c0, c1, c2, c3, out):
@@ -322,25 +315,23 @@
     wide = width // (2 * replicas)
 
     def proj(blocks, steps, sums=()):
-        return proj_call(where, keep, got_early, got_late, blocks, steps, wide, sums)
+        return proj_call(where, keep, got, blocks, steps, wide, sums)
 
     own = lax.dynamic_index_in_dim(right_basis.reshape(2, wide, rank), core, 0, keepdims=False)
     gradient, own = tie(gradient, own)
     up1, down1 = ring(own, 1), ring(own, -1)
-    (send_early,) = deal(where, gradient, wide, ((False, 0, EARLY),))
-    got_early = swap(send_early)
+    (send,) = deal(where, gradient, wide, ((False, 0, len(ORDER)),))
+    got = swap(send)
     left_got = swap(left_basis)
-    (send_late,) = deal(where, gradient, wide, ((False, EARLY, len(ORDER)),))
-    got_late = swap(send_late)
     gradient, left_got = tie(gradient, left_got)
     (keep,) = deal(where, gradient, wide, ((True, 0, len(ORDER)),))
 
-    up, down = coef_call(keep, got_early, left_basis, left_got, wide, 0, (2, 2))
+    up, down = coef_call(keep, got, left_basis, left_got, wide, 0, (2, 2))
     up1, down1, up, down = tie(up1, down1, up, down)
     up, down = shift(up, 1), shift(down, -1)
     up2, down2 = ring(up1, 1), ring(down1, -1)
-    got_late, up1, down1 = tie(got_late, up1, down1)
-    up_rest, down_rest, held = coef_call(keep, got_late, left_basis, left_got, wide, EARLY, (1, 1, 2))
+    got, up1, down1 = tie(got, up1, down1)
+    up_rest, down_rest, held = coef_call(keep, got, left_basis, left_got, wide, EARLY, (1, 1, 2))
     sums = proj([own, up1, down1], ((0, 0), (-1, 0), (1, 0)))
     up2, down2, up_rest, down_rest, *sums = tie(up2, down2, up_rest, down_rest, *sums)
 

time: 131 us -> 128 us (0.977)
  Pallas kernels: 23.2 us -> 19.8 us
  waiting for transfers between devices: 21.2 us -> 24.2 us
  local copies, waits for them, and re-layouts: 9.85 us -> 8.42 us
    pallas_call x4, Pallas kernels: 7.99 us -> 4.99 us  [proj_call(): pl.pallas_call(functools.partial(proj_kernel, wide, steps), out_shape=(sh...]
    ppermute x8, waiting for transfers between devices: 14.2 us -> 15.7 us  [ring(): return lax.ppermute(x, 'z', [(i, (i + step) % NZ) for i in range(NZ)])]
    unnamed x42 -> x30, local copies, waits for them, and re-layouts: 8.65 us -> 7.22 us
    ppermute x6 -> x5, waiting for transfers between devices: 4.35 us -> 5.37 us  [swap(): return lax.ppermute(x, 'c', [(0, 1), (1, 0)])]
    pallas_call x3 -> x2, Pallas kernels: 2.7 us -> 2.24 us  [deal(): pl.pallas_call(functools.partial(deal_kernel, wide, plans), out_shape=tup...]
    ppermute x6 -> x5, starting transfers between devices: 11.9 us -> 12.3 us  [swap(): return lax.ppermute(x, 'c', [(0, 1), (1, 0)])]
  transfers between devices with their start and end apart: 21 -> 20, of which waited for: 9 -> 12; matrix products, arithmetic and copies ran while one was open for 3% -> 3% of each run, Pallas kernels for 9% -> 6%
where the time goes in v2:
time: 128 us
  blocking collectives  36.5 us (29%)
  starting transfers between devices  34.5 us (27%)
  waiting for transfers between devices  24.2 us (19%)
  Pallas kernels  19.8 us (15%)
  local copies, waits for them, and re-layouts  8.42 us (7%)
  other arithmetic  3.67 us (3%)
    all_to_all x2, blocking collectives, everyone(): lax.all_to_all(jnp.broadcast_to(x[None], (size,) + x.shape), axes, 0, 0)  23.4 us
    ppermute x8, waiting for transfers between devices, ring(): return lax.ppermute(x, 'z', [(i, (i + step) % NZ) for i in range(NZ)])  15.7 us
    all_to_all x1, blocking collectives, local(): rows_sum = jnp.sum(lax.all_to_all(halves, ('x', 'y'), 0, 0), axis=0)  13.2 us
    ppermute x5, starting transfers between devices, swap(): return lax.ppermute(x, 'c', [(0, 1), (1, 0)])  12.3 us
    ppermute x8, starting transfers between devices, ring(): return lax.ppermute(x, 'z', [(i, (i + step) % NZ) for i in range(NZ)])  11.8 us
    pallas_call x1, Pallas kernels, final_call(): pl.pallas_call(functools.partial(final_kernel, scales), out_shape=(jax.Sh...  8.72 us
    unnamed x30, local copies, waits for them, and re-layouts  7.22 us
    ppermute x4, starting transfers between devices, shift(): return lax.ppermute(x, ('x', 'y', 'c'), pairs)  5.4 us
  transfers between devices with their start and end apart: 20, of which 12 were waited for; matrix products, arithmetic and copies ran while one was open for 3% of the time, Pallas kernels for 6%

profile of v2, /device:TPU:1, one launch (start us, length us, event | category | flops | bytes accessed | tf_op | source)
XLA Modules:
  0.0 128.0 jit_solution(665658235082566034)
XLA Ops:
  1.8 3.1 %copy-done.6 = bf16[1,256,14336]{2,1,0:T(8,128)(2,1)S(1)} copy-done((bf16[1,256,14336]{2,1,0:T(8,128)(2,1)S(1)}, bf16[1,256,14336]{2,1,0:T(8,128)(2,1)}, u32[]{:S(2)}) %copy-start.6) | copy-done | bytes 7340056
  6.0 3.3 %collective-permute-start.1 = (bf16[256,7168]{1,0:T(8,128)(2,1)S(1)}, bf16[256,7168]{1,0:T(8,128)(2,1)S(1)}, u32[]{:S(2)}, u32[]{:S(2)}) collective-permute-start(bf16[256,7168]{1,0:T(8,128)(2,1)S(1)} %deal.3), channel_id=1, source_target_pairs={{0,1},{1,0},{2,3},{3,2},{4,5},{5,4},{6,7},{7,6},{8,9},{9,8},{10,11... | collective-permute-start | bytes 11010056 | tf_op jit(solution)/shard_map/ppermute | solution.py:67
  9.3 3.9 %collective-permute-start.3 = (bf16[896,256]{1,0:T(8,128)(2,1)S(1)}, bf16[896,256]{1,0:T(8,128)(2,1)S(1)}, u32[]{:S(2)}, u32[]{:S(2)}) collective-permute-start(bf16[896,256]{1,0:T(8,128)(2,1)S(1)} %dynamic-slice_bitcast_fusion.rest_0_), channel_id=1, source_target_pairs={{0,224},{32,0},{64,32},{96,64},{128,96},{160,128},{192,160},{224,1... | collective-permute-start | bytes 1376264 | tf_op jit(solution)/shard_map/ppermute | solution.py:59
  13.5 2.0 %collective-permute-done.left_got = bf16[256,256]{1,0:T(8,128)(2,1)S(1)} collective-permute-done((bf16[256,256]{1,0:T(8,128)(2,1)S(1)}, bf16[256,256]{1,0:T(8,128)(2,1)S(1)}, u32[]{:S(2)}, u32[]{:S(2)}) %collective-permute-start) | collective-permute-done | bytes 131104 | tf_op jit(solution)/shard_map/ppermute | solution.py:67
  16.7 1.2 coef.2
  17.9 5.1 %collective-permute-done.3.rest_2_ = bf16[896,256]{1,0:T(8,128)(2,1)S(1)} collective-permute-done((bf16[896,256]{1,0:T(8,128)(2,1)S(1)}, bf16[896,256]{1,0:T(8,128)(2,1)S(1)}, u32[]{:S(2)}, u32[]{:S(2)}) %collective-permute-start.3) | collective-permute-done | bytes 458784 | tf_op jit(solution)/shard_map/ppermute | solution.py:59
  23.0 3.1 %collective-permute-done.2.rest_1_ = bf16[896,256]{1,0:T(8,128)(2,1)S(1)} collective-permute-done((bf16[896,256]{1,0:T(8,128)(2,1)S(1)}, bf16[896,256]{1,0:T(8,128)(2,1)S(1)}, u32[]{:S(2)}, u32[]{:S(2)}) %collective-permute-start.2) | collective-permute-done | bytes 458784 | tf_op jit(solution)/shard_map/ppermute | solution.py:59
  26.1 1.3 %collective-permute-start.4 = (bf16[1792,256]{1,0:T(8,128)(2,1)S(1)}, bf16[1792,256]{1,0:T(8,128)(2,1)S(1)}, u32[]{:S(2)}, u32[]{:S(2)}) collective-permute-start(bf16[1792,256]{1,0:T(8,128)(2,1)S(1)} %get-tuple-element.67), channel_id=1, source_target_pairs={{0,8},{1,3},{2,10},{3,5},{4,12},{5,7},{6,14},{7,1},{8,16},{9,11},{... | collective-permute-start | bytes 2752520 | tf_op jit(solution)/shard_map/ppermute | solution.py:46
  27.4 1.4 %collective-permute-start.5 = (bf16[1792,256]{1,0:T(8,128)(2,1)S(1)}, bf16[1792,256]{1,0:T(8,128)(2,1)S(1)}, u32[]{:S(2)}, u32[]{:S(2)}) collective-permute-start(bf16[1792,256]{1,0:T(8,128)(2,1)S(1)} %get-tuple-element.68), channel_id=1, source_target_pairs={{0,24},{1,7},{2,26},{3,1},{4,28},{5,3},{6,30},{7,5},{8,0},{9,15},{... | collective-permute-start | bytes 2752520 | tf_op jit(solution)/shard_map/ppermute | solution.py:46
  28.9 2.7 %collective-permute-start.7 = (bf16[896,256]{1,0:T(8,128)(2,1)S(1)}, bf16[896,256]{1,0:T(8,128)(2,1)S(1)}, u32[]{:S(2)}, u32[]{:S(2)}) collective-permute-start(bf16[896,256]{1,0:T(8,128)(2,1)S(1)} %collective-permute-done.3.rest_2_), channel_id=1, source_target_pairs={{0,224},{32,0},{64,32},{96,64},{128,96},{160,128},{192,160},{224,1... | collective-permute-start | bytes 1376264 | tf_op jit(solution)/shard_map/ppermute | solution.py:59
  31.5 1.2 coef.3
  32.8 1.5 %proj.4 = (f32[256,256]{1,0:T(8,128)S(1)}, f32[256,256]{1,0:T(8,128)S(1)}) custom-call(s32[4]{0:T(128)S(1)} %pad_add_fusion.where, bf16[256,7168]{1,0:T(8,128)(2,1)S(1)} %deal.2.keep, bf16[256,7168]{1,0:T(8,128)(2,1)S(1)} %collective-permute-done.1.got, bf16[896,256]{1,0:T(8,128)(2,1)S(1)} %dynamic-slice_bitcast_fusion.rest_0_, ...), custom_call_target="tpu_custom_call" | custom-call | tf_op jit(solution)/shard_map/proj/pallas_call | solution.py:175
  34.3 6.1 %collective-permute-done.6.rest_0_ = bf16[896,256]{1,0:T(8,128)(2,1)S(1)} collective-permute-done((bf16[896,256]{1,0:T(8,128)(2,1)S(1)}, bf16[896,256]{1,0:T(8,128)(2,1)S(1)}, u32[]{:S(2)}, u32[]{:S(2)}) %collective-permute-start.6) | collective-permute-done | bytes 458784 | tf_op jit(solution)/shard_map/ppermute | solution.py:59
  40.4 2.7 %collective-permute-start.11 = (bf16[896,256]{1,0:T(8,128)(2,1)S(1)}, bf16[896,256]{1,0:T(8,128)(2,1)S(1)}, u32[]{:S(2)}, u32[]{:S(2)}) collective-permute-start(bf16[896,256]{1,0:T(8,128)(2,1)S(1)} %collective-permute-done.7.rest_1_), channel_id=1, source_target_pairs={{0,224},{32,0},{64,32},{96,64},{128,96},{160,128},{192,160},{224,1... | collective-permute-start | bytes 1376264 | tf_op jit(solution)/shard_map/ppermute | solution.py:59
  44.9 2.7 %collective-permute-start.9 = (bf16[896,256]{1,0:T(8,128)(2,1)}, bf16[896,256]{1,0:T(8,128)(2,1)}, u32[]{:S(2)}, u32[]{:S(2)}) collective-permute-start(bf16[896,256]{1,0:T(8,128)(2,1)} %slice_add_fusion), channel_id=1, source_target_pairs={{0,24},{1,7},{2,26},{3,1},{4,28},{5,3},{6,30},{7,5},{8,0},{9,15},{... | collective-permute-start | bytes 1376264 | tf_op jit(solution)/shard_map/ppermute | solution.py:46
  47.5 2.0 %copy-done.1 = bf16[256,7168]{1,0:T(8,128)(2,1)S(1)} copy-done((bf16[256,7168]{1,0:T(8,128)(2,1)S(1)}, bf16[256,7168]{1,0:T(8,128)(2,1)}, u32[]{:S(2)}) %copy-start.1) | copy-done | bytes 3670040
  49.6 2.0 %copy-done.4 = bf16[256,7168]{1,0:T(8,128)(2,1)S(1)} copy-done((bf16[256,7168]{1,0:T(8,128)(2,1)S(1)}, bf16[256,7168]{1,0:T(8,128)(2,1)}, u32[]{:S(2)}) %copy-start.4) | copy-done | bytes 3670040
  51.6 1.2 proj.5
  53.3 1.7 %add_convert_fusion.1 = (bf16[896,256]{1,0:T(8,128)(2,1)S(1)}, bf16[896,256]{1,0:T(8,128)(2,1)S(1)}) fusion(bf16[896,256]{1,0:T(8,128)(2,1)} %collective-permute-done.8, bf16[1792,256]{1,0:T(8,128)(2,1)S(1)} %copy-done.14, bf16[1792,256]{1,0:T(8,128)(2,1)S(1)} %get-tuple-element.66, bf16[896,256]{1,0:T(8,128)(2,1)} %collective-permute-done.9, ...), kind=kLoop, calls=%fused_computation.2 | loop fusion | flops 2752512 | bytes 3670016 | tf_op jit(solution)/shard_map/convert
  55.1 3.8 %collective-permute-start.14 = (bf16[448,256]{1,0:T(8,128)(2,1)S(1)}, bf16[448,256]{1,0:T(8,128)(2,1)S(1)}, u32[]{:S(2)}, u32[]{:S(2)}) collective-permute-start(bf16[448,256]{1,0:T(8,128)(2,1)S(1)} %get-tuple-element.111), channel_id=1, source_target_pairs={{0,6},{1,25},{2,0},{3,27},{4,2},{5,29},{6,4},{7,31},{8,14},{9,1},{... | collective-permute-start | bytes 688136 | tf_op jit(solution)/shard_map/ppermute | solution.py:55
  60.1 2.5 %collective-permute-start.16 = (bf16[384,256]{1,0:T(8,128)(2,1)S(1)}, bf16[384,256]{1,0:T(8,128)(2,1)S(1)}, u32[]{:S(2)}, u32[]{:S(2)}) collective-permute-start(bf16[384,256]{1,0:T(8,128)(2,1)S(1)} %slice.31), channel_id=1, source_target_pairs={{0,224},{32,0},{64,32},{96,64},{128,96},{160,128},{192,160},{224,1... | collective-permute-start | bytes 589832 | tf_op jit(solution)/shard_map/ppermute | solution.py:59
  62.6 1.2 proj.6
  63.9 1.4 %collective-permute-done.16.rest_1_ = bf16[384,256]{1,0:T(8,128)(2,1)S(1)} collective-permute-done((bf16[384,256]{1,0:T(8,128)(2,1)S(1)}, bf16[384,256]{1,0:T(8,128)(2,1)S(1)}, u32[]{:S(2)}, u32[]{:S(2)}) %collective-permute-start.16) | collective-permute-done | bytes 196640 | tf_op jit(solution)/shard_map/ppermute | solution.py:59
  65.4 2.6 %collective-permute-done.12.c1 = bf16[448,256]{1,0:T(8,128)(2,1)S(1)} collective-permute-done((bf16[448,256]{1,0:T(8,128)(2,1)S(1)}, bf16[448,256]{1,0:T(8,128)(2,1)S(1)}, u32[]{:S(2)}, u32[]{:S(2)}) %collective-permute-start.12) | collective-permute-done | bytes 229408 | tf_op jit(solution)/shard_map/ppermute | solution.py:55
  69.1 4.0 %collective-permute-start.17 = (f32[256,256]{1,0:T(8,128)S(1)}, f32[256,256]{1,0:T(8,128)S(1)}, u32[]{:S(2)}, u32[]{:S(2)}) collective-permute-start(f32[256,256]{1,0:T(8,128)S(1)} %get-tuple-element.104), channel_id=1, source_target_pairs={{0,1},{1,0},{2,3},{3,2},{4,5},{5,4},{6,7},{7,6},{8,9},{9,8},{10,11... | collective-permute-start | bytes 786440 | tf_op jit(solution)/shard_map/ppermute | solution.py:67
  75.7 1.4 %collective-permute-done.18 = f32[128,768]{1,0:T(8,128)S(1)} collective-permute-done((f32[128,768]{1,0:T(8,128)S(1)}, f32[128,768]{1,0:T(8,128)S(1)}, u32[]{:S(2)}, u32[]{:S(2)}) %collective-permute-start.18) | collective-permute-done | bytes 393248 | tf_op jit(solution)/shard_map/ppermute | solution.py:67
  77.1 13.2 %all_to_all.15 = f32[16,8,768]{2,1,0:T(8,128)S(1)} all-to-all(f32[16,8,768]{2,1,0:T(8,128)S(1)} %add_bitcast_fusion), channel_id=1, replica_groups=mesh['z'=8,'x'=4,'y'=4,'c'=2] {'x','y'}, dimensions={0} | all-to-all | bytes 786432 | tf_op jit(solution)/shard_map/all_to_all | solution.py:364
  90.3 12.0 %all_to_all.16 = f32[8,8,768]{2,1,0:T(8,128)S(1)} all-to-all(f32[8,8,768]{2,1,0:T(8,128)S(1)} %broadcast_in_dim.4), channel_id=1, replica_groups=mesh['z'=8,'x'=4,'y'=4,'c'=2] {'z'}, dimensions={0} | all-to-all | bytes 393216 | tf_op jit(solution)/shard_map/all_to_all | solution.py:71
  102.4 11.3 %all_to_all.17 = f32[16,8,768]{2,1,0:T(8,128)S(1)} all-to-all(f32[16,8,768]{2,1,0:T(8,128)S(1)} %broadcast_in_dim.5), channel_id=1, replica_groups=mesh['z'=8,'x'=4,'y'=4,'c'=2] {'x','y'}, dimensions={0} | all-to-all | bytes 786432 | tf_op jit(solution)/shard_map/all_to_all | solution.py:71
  113.7 4.2 %collective-permute-start.19 = (f32[128,768]{1,0:T(8,128)S(1)}, f32[128,768]{1,0:T(8,128)S(1)}, u32[]{:S(2)}, u32[]{:S(2)}) collective-permute-start(f32[128,768]{1,0:T(8,128)S(1)} %bitcast.23), channel_id=1, source_target_pairs={{0,1},{1,0},{2,3},{3,2},{4,5},{5,4},{6,7},{7,6},{8,9},{9,8},{10,11... | collective-permute-start | bytes 1179656 | tf_op jit(solution)/shard_map/ppermute | solution.py:67
  117.9 1.3 %collective-permute-done.19.theirs = f32[128,768]{1,0:T(8,128)S(1)} collective-permute-done((f32[128,768]{1,0:T(8,128)S(1)}, f32[128,768]{1,0:T(8,128)S(1)}, u32[]{:S(2)}, u32[]{:S(2)}) %collective-permute-start.19) | collective-permute-done | bytes 393248 | tf_op jit(solution)/shard_map/ppermute | solution.py:67
  119.3 8.7 %roots_and_update.1 = (bf16[256,1792]{1,0:T(8,128)(2,1)}, f32[256,256]{1,0:T(8,128)}, f32[256,256]{1,0:T(8,128)}) custom-call(s32[4]{0:T(128)S(1)} %pad_add_fusion.where, f32[128,768]{1,0:T(8,128)S(1)} %bitcast.24, f32[128,768]{1,0:T(8,128)S(1)} %collective-permute-done.19.theirs, f32[256,256]{1,0:T(8,128)S(1)} %copy-done.9, f32[256,256]{1,0:T(8,128)S(1)} %copy-done.10, ...), custom_call_target="tpu_custom_call" | custom-call | tf_op jit(solution)/shard_map/roots_and_update/pallas_call | solution.py:291
  (66 shorter events, 11.1 us)
Async XLA Ops:
  1.8 3.1 %copy-start.6 = (bf16[1,256,14336]{2,1,0:T(8,128)(2,1)S(1)}, bf16[1,256,14336]{2,1,0:T(8,128)(2,1)}, u32[]{:S(2)}) copy-start(bf16[1,256,14336]{2,1,0:T(8,128)(2,1)} %param.5) | copy-start | bytes 22020100
  4.9 8.3 %copy-start.7 = (bf16[256,256]{1,0:T(8,128)(2,1)S(1)}, bf16[256,256]{1,0:T(8,128)(2,1)}, u32[]{:S(2)}) copy-start(bf16[256,256]{1,0:T(8,128)(2,1)} %left.7) | copy-start | bytes 393220
  6.0 10.7 %collective-permute-start.1 = (bf16[256,7168]{1,0:T(8,128)(2,1)S(1)}, bf16[256,7168]{1,0:T(8,128)(2,1)S(1)}, u32[]{:S(2)}, u32[]{:S(2)}) collective-permute-start(bf16[256,7168]{1,0:T(8,128)(2,1)S(1)} %deal.3), channel_id=1, source_target_pairs={{0,1},{1,0},{2,3},{3,2},{4,5},{5,4},{6,7},{7,6},{8,9},{9,8},{10,11... | collective-permute-start | bytes 11010056 | tf_op jit(solution)/shard_map/ppermute | solution.py:67
  9.3 13.7 %collective-permute-start.3 = (bf16[896,256]{1,0:T(8,128)(2,1)S(1)}, bf16[896,256]{1,0:T(8,128)(2,1)S(1)}, u32[]{:S(2)}, u32[]{:S(2)}) collective-permute-start(bf16[896,256]{1,0:T(8,128)(2,1)S(1)} %dynamic-slice_bitcast_fusion.rest_0_), channel_id=1, source_target_pairs={{0,224},{32,0},{64,32},{96,64},{128,96},{160,128},{192,160},{224,1... | collective-permute-start | bytes 1376264 | tf_op jit(solution)/shard_map/ppermute | solution.py:59
  13.2 13.0 %collective-permute-start.2 = (bf16[896,256]{1,0:T(8,128)(2,1)S(1)}, bf16[896,256]{1,0:T(8,128)(2,1)S(1)}, u32[]{:S(2)}, u32[]{:S(2)}) collective-permute-start(bf16[896,256]{1,0:T(8,128)(2,1)S(1)} %dynamic-slice_bitcast_fusion.rest_0_), channel_id=1, source_target_pairs={{0,32},{32,64},{64,96},{96,128},{128,160},{160,192},{192,224},{224... | collective-permute-start | bytes 1376264 | tf_op jit(solution)/shard_map/ppermute | solution.py:59
  13.2 2.4 %collective-permute-start = (bf16[256,256]{1,0:T(8,128)(2,1)S(1)}, bf16[256,256]{1,0:T(8,128)(2,1)S(1)}, u32[]{:S(2)}, u32[]{:S(2)}) collective-permute-start(bf16[256,256]{1,0:T(8,128)(2,1)S(1)} %copy-done.7), channel_id=1, source_target_pairs={{0,1},{1,0},{2,3},{3,2},{4,5},{5,4},{6,7},{7,6},{8,9},{9,8},{10,11... | collective-permute-start | bytes 393224 | tf_op jit(solution)/shard_map/ppermute | solution.py:67
  16.7 16.1 %copy-start = (bf16[256,7168]{1,0:T(8,128)(2,1)}, bf16[256,7168]{1,0:T(8,128)(2,1)S(1)}, u32[]{:S(2)}) copy-start(bf16[256,7168]{1,0:T(8,128)(2,1)S(1)} %deal.2.keep) | copy-start | bytes 11010052
  16.7 16.1 %copy-start.3 = (bf16[256,7168]{1,0:T(8,128)(2,1)}, bf16[256,7168]{1,0:T(8,128)(2,1)S(1)}, u32[]{:S(2)}) copy-start(bf16[256,7168]{1,0:T(8,128)(2,1)S(1)} %collective-permute-done.1.got) | copy-start | bytes 11010052
  26.1 16.9 %collective-permute-start.4 = (bf16[1792,256]{1,0:T(8,128)(2,1)S(1)}, bf16[1792,256]{1,0:T(8,128)(2,1)S(1)}, u32[]{:S(2)}, u32[]{:S(2)}) collective-permute-start(bf16[1792,256]{1,0:T(8,128)(2,1)S(1)} %get-tuple-element.67), channel_id=1, source_target_pairs={{0,8},{1,3},{2,10},{3,5},{4,12},{5,7},{6,14},{7,1},{8,16},{9,11},{... | collective-permute-start | bytes 2752520 | tf_op jit(solution)/shard_map/ppermute | solution.py:46
  27.4 15.7 %collective-permute-start.5 = (bf16[1792,256]{1,0:T(8,128)(2,1)S(1)}, bf16[1792,256]{1,0:T(8,128)(2,1)S(1)}, u32[]{:S(2)}, u32[]{:S(2)}) collective-permute-start(bf16[1792,256]{1,0:T(8,128)(2,1)S(1)} %get-tuple-element.68), channel_id=1, source_target_pairs={{0,24},{1,7},{2,26},{3,1},{4,28},{5,3},{6,30},{7,5},{8,0},{9,15},{... | collective-permute-start | bytes 2752520 | tf_op jit(solution)/shard_map/ppermute | solution.py:46
  28.9 11.5 %collective-permute-start.6 = (bf16[896,256]{1,0:T(8,128)(2,1)S(1)}, bf16[896,256]{1,0:T(8,128)(2,1)S(1)}, u32[]{:S(2)}, u32[]{:S(2)}) collective-permute-start(bf16[896,256]{1,0:T(8,128)(2,1)S(1)} %collective-permute-done.2.rest_1_), channel_id=1, source_target_pairs={{0,32},{32,64},{64,96},{96,128},{128,160},{160,192},{192,224},{224... | collective-permute-start | bytes 1376264 | tf_op jit(solution)/shard_map/ppermute | solution.py:59
  28.9 11.5 %collective-permute-start.7 = (bf16[896,256]{1,0:T(8,128)(2,1)S(1)}, bf16[896,256]{1,0:T(8,128)(2,1)S(1)}, u32[]{:S(2)}, u32[]{:S(2)}) collective-permute-start(bf16[896,256]{1,0:T(8,128)(2,1)S(1)} %collective-permute-done.3.rest_2_), channel_id=1, source_target_pairs={{0,224},{32,0},{64,32},{96,64},{128,96},{160,128},{192,160},{224,1... | collective-permute-start | bytes 1376264 | tf_op jit(solution)/shard_map/ppermute | solution.py:59
  40.4 12.5 %collective-permute-start.10 = (bf16[896,256]{1,0:T(8,128)(2,1)S(1)}, bf16[896,256]{1,0:T(8,128)(2,1)S(1)}, u32[]{:S(2)}, u32[]{:S(2)}) collective-permute-start(bf16[896,256]{1,0:T(8,128)(2,1)S(1)} %collective-permute-done.6.rest_0_), channel_id=1, source_target_pairs={{0,32},{32,64},{64,96},{96,128},{128,160},{160,192},{192,224},{224... | collective-permute-start | bytes 1376264 | tf_op jit(solution)/shard_map/ppermute | solution.py:59
  40.4 12.5 %collective-permute-start.11 = (bf16[896,256]{1,0:T(8,128)(2,1)S(1)}, bf16[896,256]{1,0:T(8,128)(2,1)S(1)}, u32[]{:S(2)}, u32[]{:S(2)}) collective-permute-start(bf16[896,256]{1,0:T(8,128)(2,1)S(1)} %collective-permute-done.7.rest_1_), channel_id=1, source_target_pairs={{0,224},{32,0},{64,32},{96,64},{128,96},{160,128},{192,160},{224,1... | collective-permute-start | bytes 1376264 | tf_op jit(solution)/shard_map/ppermute | solution.py:59
  43.1 1.8 %copy-start.11 = (bf16[1792,256]{1,0:T(8,128)(2,1)}, bf16[1792,256]{1,0:T(8,128)(2,1)S(1)}, u32[]{:S(2)}) copy-start(bf16[1792,256]{1,0:T(8,128)(2,1)S(1)} %collective-permute-done.4) | copy-start | bytes 2752516
  44.0 9.2 %collective-permute-start.8 = (bf16[896,256]{1,0:T(8,128)(2,1)}, bf16[896,256]{1,0:T(8,128)(2,1)}, u32[]{:S(2)}, u32[]{:S(2)}) collective-permute-start(bf16[896,256]{1,0:T(8,128)(2,1)} %slice_add_fusion.1), channel_id=1, source_target_pairs={{0,8},{1,3},{2,10},{3,5},{4,12},{5,7},{6,14},{7,1},{8,16},{9,11},{... | collective-permute-start | bytes 1376264 | tf_op jit(solution)/shard_map/ppermute | solution.py:46
  44.9 8.4 %collective-permute-start.9 = (bf16[896,256]{1,0:T(8,128)(2,1)}, bf16[896,256]{1,0:T(8,128)(2,1)}, u32[]{:S(2)}, u32[]{:S(2)}) collective-permute-start(bf16[896,256]{1,0:T(8,128)(2,1)} %slice_add_fusion), channel_id=1, source_target_pairs={{0,24},{1,7},{2,26},{3,1},{4,28},{5,3},{6,30},{7,5},{8,0},{9,15},{... | collective-permute-start | bytes 1376264 | tf_op jit(solution)/shard_map/ppermute | solution.py:46
  47.5 2.0 %copy-start.1 = (bf16[256,7168]{1,0:T(8,128)(2,1)S(1)}, bf16[256,7168]{1,0:T(8,128)(2,1)}, u32[]{:S(2)}) copy-start(bf16[256,7168]{1,0:T(8,128)(2,1)} %copy-done) | copy-start | bytes 11010052
  49.6 2.0 %copy-start.4 = (bf16[256,7168]{1,0:T(8,128)(2,1)S(1)}, bf16[256,7168]{1,0:T(8,128)(2,1)}, u32[]{:S(2)}) copy-start(bf16[256,7168]{1,0:T(8,128)(2,1)} %copy-done.3) | copy-start | bytes 11010052
  52.9 12.3 %collective-permute-start.15 = (bf16[512,256]{1,0:T(8,128)(2,1)S(1)}, bf16[512,256]{1,0:T(8,128)(2,1)S(1)}, u32[]{:S(2)}, u32[]{:S(2)}) collective-permute-start(bf16[512,256]{1,0:T(8,128)(2,1)S(1)} %slice.30), channel_id=1, source_target_pairs={{0,32},{32,64},{64,96},{96,128},{128,160},{160,192},{192,224},{224... | collective-permute-start | bytes 786440 | tf_op jit(solution)/shard_map/ppermute | solution.py:59
  53.3 9.3 %copy-start.2 = (bf16[256,7168]{1,0:T(8,128)(2,1)S(1)}, bf16[256,7168]{1,0:T(8,128)(2,1)}, u32[]{:S(2)}) copy-start(bf16[256,7168]{1,0:T(8,128)(2,1)} %copy-done) | copy-start | bytes 11010052
  53.3 9.3 %copy-start.5 = (bf16[256,7168]{1,0:T(8,128)(2,1)S(1)}, bf16[256,7168]{1,0:T(8,128)(2,1)}, u32[]{:S(2)}) copy-start(bf16[256,7168]{1,0:T(8,128)(2,1)} %copy-done.3) | copy-start | bytes 11010052
  55.1 10.1 %collective-permute-start.14 = (bf16[448,256]{1,0:T(8,128)(2,1)S(1)}, bf16[448,256]{1,0:T(8,128)(2,1)S(1)}, u32[]{:S(2)}, u32[]{:S(2)}) collective-permute-start(bf16[448,256]{1,0:T(8,128)(2,1)S(1)} %get-tuple-element.111), channel_id=1, source_target_pairs={{0,6},{1,25},{2,0},{3,27},{4,2},{5,29},{6,4},{7,31},{8,14},{9,1},{... | collective-permute-start | bytes 688136 | tf_op jit(solution)/shard_map/ppermute | solution.py:55
  59.0 6.5 %collective-permute-start.13 = (bf16[448,256]{1,0:T(8,128)(2,1)S(1)}, bf16[448,256]{1,0:T(8,128)(2,1)S(1)}, u32[]{:S(2)}, u32[]{:S(2)}) collective-permute-start(bf16[448,256]{1,0:T(8,128)(2,1)S(1)} %get-tuple-element.112), channel_id=1, source_target_pairs={{0,4},{1,17},{2,6},{3,19},{4,0},{5,21},{6,2},{7,23},{8,12},{9,25},... | collective-permute-start | bytes 688136 | tf_op jit(solution)/shard_map/ppermute | solution.py:55
  59.5 8.6 %collective-permute-start.12 = (bf16[448,256]{1,0:T(8,128)(2,1)S(1)}, bf16[448,256]{1,0:T(8,128)(2,1)S(1)}, u32[]{:S(2)}, u32[]{:S(2)}) collective-permute-start(bf16[448,256]{1,0:T(8,128)(2,1)S(1)} %get-tuple-element.113), channel_id=1, source_target_pairs={{0,2},{1,9},{2,4},{3,11},{4,6},{5,13},{6,0},{7,15},{8,10},{9,17},{... | collective-permute-start | bytes 688136 | tf_op jit(solution)/shard_map/ppermute | solution.py:55
  60.1 5.1 %collective-permute-start.16 = (bf16[384,256]{1,0:T(8,128)(2,1)S(1)}, bf16[384,256]{1,0:T(8,128)(2,1)S(1)}, u32[]{:S(2)}, u32[]{:S(2)}) collective-permute-start(bf16[384,256]{1,0:T(8,128)(2,1)S(1)} %slice.31), channel_id=1, source_target_pairs={{0,224},{32,0},{64,32},{96,64},{128,96},{160,128},{192,160},{224,1... | collective-permute-start | bytes 589832 | tf_op jit(solution)/shard_map/ppermute | solution.py:59
  69.1 50.2 %copy-start.8 = (bf16[1792,256]{1,0:T(8,128)(2,1)S(1)}, bf16[1792,256]{1,0:T(8,128)(2,1)}, u32[]{:S(2)}) copy-start(bf16[1792,256]{1,0:T(8,128)(2,1)} %right.1) | copy-start | bytes 2752516
  69.1 50.2 %copy-start.9 = (f32[256,256]{1,0:T(8,128)S(1)}, f32[256,256]{1,0:T(8,128)}, u32[]{:S(2)}) copy-start(f32[256,256]{1,0:T(8,128)} %left_stat.1) | copy-start | bytes 786436
  69.1 50.2 %copy-start.10 = (f32[256,256]{1,0:T(8,128)S(1)}, f32[256,256]{1,0:T(8,128)}, u32[]{:S(2)}) copy-start(f32[256,256]{1,0:T(8,128)} %right_stat.1) | copy-start | bytes 786436
  69.1 5.1 %collective-permute-start.17 = (f32[256,256]{1,0:T(8,128)S(1)}, f32[256,256]{1,0:T(8,128)S(1)}, u32[]{:S(2)}, u32[]{:S(2)}) collective-permute-start(f32[256,256]{1,0:T(8,128)S(1)} %get-tuple-element.104), channel_id=1, source_target_pairs={{0,1},{1,0},{2,3},{3,2},{4,5},{5,4},{6,7},{7,6},{8,9},{9,8},{10,11... | collective-permute-start | bytes 786440 | tf_op jit(solution)/shard_map/ppermute | solution.py:67
  75.2 1.8 %collective-permute-start.18 = (f32[128,768]{1,0:T(8,128)S(1)}, f32[128,768]{1,0:T(8,128)S(1)}, u32[]{:S(2)}, u32[]{:S(2)}) collective-permute-start(f32[128,768]{1,0:T(8,128)S(1)} %get-tuple-element.110), channel_id=1, source_target_pairs={{0,1},{1,0},{2,3},{3,2},{4,5},{5,4},{6,7},{7,6},{8,9},{9,8},{10,11... | collective-permute-start | bytes 1179656 | tf_op jit(solution)/shard_map/ppermute | solution.py:67
  113.7 5.6 %collective-permute-start.19 = (f32[128,768]{1,0:T(8,128)S(1)}, f32[128,768]{1,0:T(8,128)S(1)}, u32[]{:S(2)}, u32[]{:S(2)}) collective-permute-start(f32[128,768]{1,0:T(8,128)S(1)} %bitcast.23), channel_id=1, source_target_pairs={{0,1},{1,0},{2,3},{3,2},{4,5},{5,4},{6,7},{7,6},{8,9},{9,8},{10,11... | collective-permute-start | bytes 1179656 | tf_op jit(solution)/shard_map/ppermute | solution.py:67
  (3 other events, 5.1 us)

commit v3 on v2

--- a/solution.py
+++ b/solution.py
@@ -107,7 +107,7 @@
         item.wait()
 
 
-def deal(where, grad, wide, plans):
+def deal(where, grad, wide, plans, grant):
     rows = grad.shape[0]
     count = sum(high - low for _, low, high in plans)
     vmem = pl.BlockSpec(memory_space=pltpu.VMEM)
@@ -117,7 +117,7 @@
         in_specs=[pl.BlockSpec(memory_space=pltpu.SMEM), pl.BlockSpec(memory_space=pltpu.HBM)],
         out_specs=tuple(vmem for _ in plans),
         scratch_shapes=[pltpu.SemaphoreType.DMA((count,))],
-        compiler_params=params(10),
+        compiler_params=params(grant),
         name="deal",
     )(where, grad)
 
@@ -320,11 +320,11 @@
     own = lax.dynamic_index_in_dim(right_basis.reshape(2, wide, rank), core, 0, keepdims=False)
     gradient, own = tie(gradient, own)
     up1, down1 = ring(own, 1), ring(own, -1)
-    (send,) = deal(where, gradient, wide, ((False, 0, len(ORDER)),))
+    (send,) = deal(where, gradient, wide, ((False, 0, len(ORDER)),), 52)
     got = swap(send)
     left_got = swap(left_basis)
     gradient, left_got = tie(gradient, left_got)
-    (keep,) = deal(where, gradient, wide, ((True, 0, len(ORDER)),))
+    (keep,) = deal(where, gradient, wide, ((True, 0, len(ORDER)),), 10)
 
     up, down = coef_call(keep, got, left_basis, left_got, wide, 0, (2, 2))
     up1, down1, up, down = tie(up1, down1, up, down)

time: 128 us -> 129 us (level)
  Pallas kernels: 19.8 us -> 23.4 us
  local copies, waits for them, and re-layouts: 8.42 us -> 5.34 us
    pallas_call x2, Pallas kernels: 2.24 us -> 5.8 us  [deal(): pl.pallas_call(functools.partial(deal_kernel, wide, plans), out_shape=tup...]
    unnamed x30, local copies, waits for them, and re-layouts: 7.22 us -> 4.14 us
where the time goes in v3:
time: 129 us
  blocking collectives  36.5 us (28%)
  starting transfers between devices  34.5 us (27%)
  waiting for transfers between devices  24.2 us (19%)
  Pallas kernels  23.4 us (18%)
  local copies, waits for them, and re-layouts  5.34 us (4%)
  other arithmetic  3.73 us (3%)
    all_to_all x2, blocking collectives, everyone(): lax.all_to_all(jnp.broadcast_to(x[None], (size,) + x.shape), axes, 0, 0)  23.4 us
    ppermute x8, waiting for transfers between devices, ring(): return lax.ppermute(x, 'z', [(i, (i + step) % NZ) for i in range(NZ)])  15.7 us
    all_to_all x1, blocking collectives, local(): rows_sum = jnp.sum(lax.all_to_all(halves, ('x', 'y'), 0, 0), axis=0)  13.2 us
    ppermute x5, starting transfers between devices, swap(): return lax.ppermute(x, 'c', [(0, 1), (1, 0)])  12.3 us
    ppermute x8, starting transfers between devices, ring(): return lax.ppermute(x, 'z', [(i, (i + step) % NZ) for i in range(NZ)])  11.8 us
    pallas_call x1, Pallas kernels, final_call(): pl.pallas_call(functools.partial(final_kernel, scales), out_shape=(jax.Sh...  8.72 us
    pallas_call x2, Pallas kernels, deal(): pl.pallas_call(functools.partial(deal_kernel, wide, plans), out_shape=tup...  5.8 us
    ppermute x4, starting transfers between devices, shift(): return lax.ppermute(x, ('x', 'y', 'c'), pairs)  5.41 us
  transfers between devices with their start and end apart: 20, of which 12 were waited for; matrix products, arithmetic and copies ran while one was open for 3% of the time, Pallas kernels for 6%

profile of v3, /device:TPU:1, one launch (start us, length us, event | category | flops | bytes accessed | tf_op | source)
XLA Modules:
  0.0 128.6 jit_solution(5152800035651250953)
XLA Ops:
  1.8 4.7 %deal.3 = bf16[256,7168]{1,0:T(8,128)(2,1)} custom-call(s32[4]{0:T(128)S(1)} %pad_add_fusion.where, bf16[256,14336]{1,0:T(8,128)(2,1)} %bitcast.20), custom_call_target="tpu_custom_call" | custom-call | tf_op jit(solution)/shard_map/deal/pallas_call | solution.py:114
  6.5 3.3 %collective-permute-start.1 = (bf16[256,7168]{1,0:T(8,128)(2,1)}, bf16[256,7168]{1,0:T(8,128)(2,1)S(1)}, u32[]{:S(2)}, u32[]{:S(2)}) collective-permute-start(bf16[256,7168]{1,0:T(8,128)(2,1)} %deal.3), channel_id=1, source_target_pairs={{0,1},{1,0},{2,3},{3,2},{4,5},{5,4},{6,7},{7,6},{8,9},{9,8},{10,11... | collective-permute-start | bytes 11010056 | tf_op jit(solution)/shard_map/ppermute | solution.py:67
  9.8 3.9 %collective-permute-start.3 = (bf16[896,256]{1,0:T(8,128)(2,1)S(1)}, bf16[896,256]{1,0:T(8,128)(2,1)S(1)}, u32[]{:S(2)}, u32[]{:S(2)}) collective-permute-start(bf16[896,256]{1,0:T(8,128)(2,1)S(1)} %dynamic-slice_bitcast_fusion.rest_0_), channel_id=1, source_target_pairs={{0,224},{32,0},{64,32},{96,64},{128,96},{160,128},{192,160},{224,1... | collective-permute-start | bytes 1376264 | tf_op jit(solution)/shard_map/ppermute | solution.py:59
  14.0 2.0 %collective-permute-done.left_got = bf16[256,256]{1,0:T(8,128)(2,1)S(1)} collective-permute-done((bf16[256,256]{1,0:T(8,128)(2,1)S(1)}, bf16[256,256]{1,0:T(8,128)(2,1)S(1)}, u32[]{:S(2)}, u32[]{:S(2)}) %collective-permute-start) | collective-permute-done | bytes 131104 | tf_op jit(solution)/shard_map/ppermute | solution.py:67
  17.2 1.2 coef.2
  18.4 5.1 %collective-permute-done.3.rest_2_ = bf16[896,256]{1,0:T(8,128)(2,1)S(1)} collective-permute-done((bf16[896,256]{1,0:T(8,128)(2,1)S(1)}, bf16[896,256]{1,0:T(8,128)(2,1)S(1)}, u32[]{:S(2)}, u32[]{:S(2)}) %collective-permute-start.3) | collective-permute-done | bytes 458784 | tf_op jit(solution)/shard_map/ppermute | solution.py:59
  23.5 3.1 %collective-permute-done.2.rest_1_ = bf16[896,256]{1,0:T(8,128)(2,1)S(1)} collective-permute-done((bf16[896,256]{1,0:T(8,128)(2,1)S(1)}, bf16[896,256]{1,0:T(8,128)(2,1)S(1)}, u32[]{:S(2)}, u32[]{:S(2)}) %collective-permute-start.2) | collective-permute-done | bytes 458784 | tf_op jit(solution)/shard_map/ppermute | solution.py:59
  26.6 1.3 %collective-permute-start.4 = (bf16[1792,256]{1,0:T(8,128)(2,1)S(1)}, bf16[1792,256]{1,0:T(8,128)(2,1)S(1)}, u32[]{:S(2)}, u32[]{:S(2)}) collective-permute-start(bf16[1792,256]{1,0:T(8,128)(2,1)S(1)} %get-tuple-element.67), channel_id=1, source_target_pairs={{0,8},{1,3},{2,10},{3,5},{4,12},{5,7},{6,14},{7,1},{8,16},{9,11},{... | collective-permute-start | bytes 2752520 | tf_op jit(solution)/shard_map/ppermute | solution.py:46
  27.9 1.4 %collective-permute-start.5 = (bf16[1792,256]{1,0:T(8,128)(2,1)S(1)}, bf16[1792,256]{1,0:T(8,128)(2,1)S(1)}, u32[]{:S(2)}, u32[]{:S(2)}) collective-permute-start(bf16[1792,256]{1,0:T(8,128)(2,1)S(1)} %get-tuple-element.68), channel_id=1, source_target_pairs={{0,24},{1,7},{2,26},{3,1},{4,28},{5,3},{6,30},{7,5},{8,0},{9,15},{... | collective-permute-start | bytes 2752520 | tf_op jit(solution)/shard_map/ppermute | solution.py:46
  29.4 2.7 %collective-permute-start.7 = (bf16[896,256]{1,0:T(8,128)(2,1)S(1)}, bf16[896,256]{1,0:T(8,128)(2,1)S(1)}, u32[]{:S(2)}, u32[]{:S(2)}) collective-permute-start(bf16[896,256]{1,0:T(8,128)(2,1)S(1)} %collective-permute-done.3.rest_2_), channel_id=1, source_target_pairs={{0,224},{32,0},{64,32},{96,64},{128,96},{160,128},{192,160},{224,1... | collective-permute-start | bytes 1376264 | tf_op jit(solution)/shard_map/ppermute | solution.py:59
  32.0 1.2 coef.3
  33.3 1.5 %proj.4 = (f32[256,256]{1,0:T(8,128)S(1)}, f32[256,256]{1,0:T(8,128)S(1)}) custom-call(s32[4]{0:T(128)S(1)} %pad_add_fusion.where, bf16[256,7168]{1,0:T(8,128)(2,1)S(1)} %deal.2.keep, bf16[256,7168]{1,0:T(8,128)(2,1)S(1)} %collective-permute-done.1.got, bf16[896,256]{1,0:T(8,128)(2,1)S(1)} %dynamic-slice_bitcast_fusion.rest_0_, ...), custom_call_target="tpu_custom_call" | custom-call | tf_op jit(solution)/shard_map/proj/pallas_call | solution.py:175
  34.8 6.1 %collective-permute-done.6.rest_0_ = bf16[896,256]{1,0:T(8,128)(2,1)S(1)} collective-permute-done((bf16[896,256]{1,0:T(8,128)(2,1)S(1)}, bf16[896,256]{1,0:T(8,128)(2,1)S(1)}, u32[]{:S(2)}, u32[]{:S(2)}) %collective-permute-start.6) | collective-permute-done | bytes 458784 | tf_op jit(solution)/shard_map/ppermute | solution.py:59
  40.9 2.7 %collective-permute-start.11 = (bf16[896,256]{1,0:T(8,128)(2,1)S(1)}, bf16[896,256]{1,0:T(8,128)(2,1)S(1)}, u32[]{:S(2)}, u32[]{:S(2)}) collective-permute-start(bf16[896,256]{1,0:T(8,128)(2,1)S(1)} %collective-permute-done.7.rest_1_), channel_id=1, source_target_pairs={{0,224},{32,0},{64,32},{96,64},{128,96},{160,128},{192,160},{224,1... | collective-permute-start | bytes 1376264 | tf_op jit(solution)/shard_map/ppermute | solution.py:59
  45.4 2.7 %collective-permute-start.9 = (bf16[896,256]{1,0:T(8,128)(2,1)}, bf16[896,256]{1,0:T(8,128)(2,1)}, u32[]{:S(2)}, u32[]{:S(2)}) collective-permute-start(bf16[896,256]{1,0:T(8,128)(2,1)} %slice_add_fusion), channel_id=1, source_target_pairs={{0,24},{1,7},{2,26},{3,1},{4,28},{5,3},{6,30},{7,5},{8,0},{9,15},{... | collective-permute-start | bytes 1376264 | tf_op jit(solution)/shard_map/ppermute | solution.py:46
  48.1 2.0 %copy-done.1 = bf16[256,7168]{1,0:T(8,128)(2,1)S(1)} copy-done((bf16[256,7168]{1,0:T(8,128)(2,1)S(1)}, bf16[256,7168]{1,0:T(8,128)(2,1)}, u32[]{:S(2)}) %copy-start.1) | copy-done | bytes 3670040
  50.1 2.0 %copy-done.4 = bf16[256,7168]{1,0:T(8,128)(2,1)S(1)} copy-done((bf16[256,7168]{1,0:T(8,128)(2,1)S(1)}, bf16[256,7168]{1,0:T(8,128)(2,1)}, u32[]{:S(2)}) %copy-start.4) | copy-done | bytes 3670040
  52.2 1.2 proj.5
  53.8 1.7 %add_convert_fusion.1 = (bf16[896,256]{1,0:T(8,128)(2,1)S(1)}, bf16[896,256]{1,0:T(8,128)(2,1)S(1)}) fusion(bf16[896,256]{1,0:T(8,128)(2,1)} %collective-permute-done.8, bf16[1792,256]{1,0:T(8,128)(2,1)S(1)} %copy-done.14, bf16[1792,256]{1,0:T(8,128)(2,1)S(1)} %get-tuple-element.66, bf16[896,256]{1,0:T(8,128)(2,1)} %collective-permute-done.9, ...), kind=kLoop, calls=%fused_computation.2 | loop fusion | flops 2752512 | bytes 3670016 | tf_op jit(solution)/shard_map/convert
  55.7 3.8 %collective-permute-start.14 = (bf16[448,256]{1,0:T(8,128)(2,1)S(1)}, bf16[448,256]{1,0:T(8,128)(2,1)S(1)}, u32[]{:S(2)}, u32[]{:S(2)}) collective-permute-start(bf16[448,256]{1,0:T(8,128)(2,1)S(1)} %get-tuple-element.111), channel_id=1, source_target_pairs={{0,6},{1,25},{2,0},{3,27},{4,2},{5,29},{6,4},{7,31},{8,14},{9,1},{... | collective-permute-start | bytes 688136 | tf_op jit(solution)/shard_map/ppermute | solution.py:55
  60.7 2.5 %collective-permute-start.16 = (bf16[384,256]{1,0:T(8,128)(2,1)S(1)}, bf16[384,256]{1,0:T(8,128)(2,1)S(1)}, u32[]{:S(2)}, u32[]{:S(2)}) collective-permute-start(bf16[384,256]{1,0:T(8,128)(2,1)S(1)} %slice.31), channel_id=1, source_target_pairs={{0,224},{32,0},{64,32},{96,64},{128,96},{160,128},{192,160},{224,1... | collective-permute-start | bytes 589832 | tf_op jit(solution)/shard_map/ppermute | solution.py:59
  63.2 1.2 proj.6
  64.4 1.4 %collective-permute-done.16.rest_1_ = bf16[384,256]{1,0:T(8,128)(2,1)S(1)} collective-permute-done((bf16[384,256]{1,0:T(8,128)(2,1)S(1)}, bf16[384,256]{1,0:T(8,128)(2,1)S(1)}, u32[]{:S(2)}, u32[]{:S(2)}) %collective-permute-start.16) | collective-permute-done | bytes 196640 | tf_op jit(solution)/shard_map/ppermute | solution.py:59
  66.0 2.6 %collective-permute-done.12.c1 = bf16[448,256]{1,0:T(8,128)(2,1)S(1)} collective-permute-done((bf16[448,256]{1,0:T(8,128)(2,1)S(1)}, bf16[448,256]{1,0:T(8,128)(2,1)S(1)}, u32[]{:S(2)}, u32[]{:S(2)}) %collective-permute-start.12) | collective-permute-done | bytes 229408 | tf_op jit(solution)/shard_map/ppermute | solution.py:55
  69.7 4.0 %collective-permute-start.17 = (f32[256,256]{1,0:T(8,128)S(1)}, f32[256,256]{1,0:T(8,128)S(1)}, u32[]{:S(2)}, u32[]{:S(2)}) collective-permute-start(f32[256,256]{1,0:T(8,128)S(1)} %get-tuple-element.104), channel_id=1, source_target_pairs={{0,1},{1,0},{2,3},{3,2},{4,5},{5,4},{6,7},{7,6},{8,9},{9,8},{10,11... | collective-permute-start | bytes 786440 | tf_op jit(solution)/shard_map/ppermute | solution.py:67
  76.2 1.3 %collective-permute-done.18 = f32[128,768]{1,0:T(8,128)S(1)} collective-permute-done((f32[128,768]{1,0:T(8,128)S(1)}, f32[128,768]{1,0:T(8,128)S(1)}, u32[]{:S(2)}, u32[]{:S(2)}) %collective-permute-start.18) | collective-permute-done | bytes 393248 | tf_op jit(solution)/shard_map/ppermute | solution.py:67
  77.6 13.2 %all_to_all.15 = f32[16,8,768]{2,1,0:T(8,128)S(1)} all-to-all(f32[16,8,768]{2,1,0:T(8,128)S(1)} %add_bitcast_fusion), channel_id=1, replica_groups=mesh['z'=8,'x'=4,'y'=4,'c'=2] {'x','y'}, dimensions={0} | all-to-all | bytes 786432 | tf_op jit(solution)/shard_map/all_to_all | solution.py:364
  90.8 12.0 %all_to_all.16 = f32[8,8,768]{2,1,0:T(8,128)S(1)} all-to-all(f32[8,8,768]{2,1,0:T(8,128)S(1)} %broadcast_in_dim.4), channel_id=1, replica_groups=mesh['z'=8,'x'=4,'y'=4,'c'=2] {'z'}, dimensions={0} | all-to-all | bytes 393216 | tf_op jit(solution)/shard_map/all_to_all | solution.py:71
  102.9 11.3 %all_to_all.17 = f32[16,8,768]{2,1,0:T(8,128)S(1)} all-to-all(f32[16,8,768]{2,1,0:T(8,128)S(1)} %broadcast_in_dim.5), channel_id=1, replica_groups=mesh['z'=8,'x'=4,'y'=4,'c'=2] {'x','y'}, dimensions={0} | all-to-all | bytes 786432 | tf_op jit(solution)/shard_map/all_to_all | solution.py:71
  114.3 4.2 %collective-permute-start.19 = (f32[128,768]{1,0:T(8,128)S(1)}, f32[128,768]{1,0:T(8,128)S(1)}, u32[]{:S(2)}, u32[]{:S(2)}) collective-permute-start(f32[128,768]{1,0:T(8,128)S(1)} %bitcast.23), channel_id=1, source_target_pairs={{0,1},{1,0},{2,3},{3,2},{4,5},{5,4},{6,7},{7,6},{8,9},{9,8},{10,11... | collective-permute-start | bytes 1179656 | tf_op jit(solution)/shard_map/ppermute | solution.py:67
  118.5 1.3 %collective-permute-done.19.theirs = f32[128,768]{1,0:T(8,128)S(1)} collective-permute-done((f32[128,768]{1,0:T(8,128)S(1)}, f32[128,768]{1,0:T(8,128)S(1)}, u32[]{:S(2)}, u32[]{:S(2)}) %collective-permute-start.19) | collective-permute-done | bytes 393248 | tf_op jit(solution)/shard_map/ppermute | solution.py:67
  119.8 8.7 %roots_and_update.1 = (bf16[256,1792]{1,0:T(8,128)(2,1)}, f32[256,256]{1,0:T(8,128)}, f32[256,256]{1,0:T(8,128)}) custom-call(s32[4]{0:T(128)S(1)} %pad_add_fusion.where, f32[128,768]{1,0:T(8,128)S(1)} %bitcast.24, f32[128,768]{1,0:T(8,128)S(1)} %collective-permute-done.19.theirs, f32[256,256]{1,0:T(8,128)S(1)} %copy-done.9, f32[256,256]{1,0:T(8,128)S(1)} %copy-done.10, ...), custom_call_target="tpu_custom_call" | custom-call | tf_op jit(solution)/shard_map/roots_and_update/pallas_call | solution.py:291
  (66 shorter events, 10.1 us)
Async XLA Ops:
  1.8 11.9 %copy-start.7 = (bf16[256,256]{1,0:T(8,128)(2,1)S(1)}, bf16[256,256]{1,0:T(8,128)(2,1)}, u32[]{:S(2)}) copy-start(bf16[256,256]{1,0:T(8,128)(2,1)} %left.7) | copy-start | bytes 393220
  1.8 14.2 %copy-start.6 = (bf16[1,256,14336]{2,1,0:T(8,128)(2,1)S(1)}, bf16[1,256,14336]{2,1,0:T(8,128)(2,1)}, u32[]{:S(2)}) copy-start(bf16[1,256,14336]{2,1,0:T(8,128)(2,1)} %param.5) | copy-start | bytes 22020100
  6.5 10.7 %collective-permute-start.1 = (bf16[256,7168]{1,0:T(8,128)(2,1)}, bf16[256,7168]{1,0:T(8,128)(2,1)S(1)}, u32[]{:S(2)}, u32[]{:S(2)}) collective-permute-start(bf16[256,7168]{1,0:T(8,128)(2,1)} %deal.3), channel_id=1, source_target_pairs={{0,1},{1,0},{2,3},{3,2},{4,5},{5,4},{6,7},{7,6},{8,9},{9,8},{10,11... | collective-permute-start | bytes 11010056 | tf_op jit(solution)/shard_map/ppermute | solution.py:67
  9.8 13.7 %collective-permute-start.3 = (bf16[896,256]{1,0:T(8,128)(2,1)S(1)}, bf16[896,256]{1,0:T(8,128)(2,1)S(1)}, u32[]{:S(2)}, u32[]{:S(2)}) collective-permute-start(bf16[896,256]{1,0:T(8,128)(2,1)S(1)} %dynamic-slice_bitcast_fusion.rest_0_), channel_id=1, source_target_pairs={{0,224},{32,0},{64,32},{96,64},{128,96},{160,128},{192,160},{224,1... | collective-permute-start | bytes 1376264 | tf_op jit(solution)/shard_map/ppermute | solution.py:59
  13.7 13.0 %collective-permute-start.2 = (bf16[896,256]{1,0:T(8,128)(2,1)S(1)}, bf16[896,256]{1,0:T(8,128)(2,1)S(1)}, u32[]{:S(2)}, u32[]{:S(2)}) collective-permute-start(bf16[896,256]{1,0:T(8,128)(2,1)S(1)} %dynamic-slice_bitcast_fusion.rest_0_), channel_id=1, source_target_pairs={{0,32},{32,64},{64,96},{96,128},{128,160},{160,192},{192,224},{224... | collective-permute-start | bytes 1376264 | tf_op jit(solution)/shard_map/ppermute | solution.py:59
  13.7 2.4 %collective-permute-start = (bf16[256,256]{1,0:T(8,128)(2,1)S(1)}, bf16[256,256]{1,0:T(8,128)(2,1)S(1)}, u32[]{:S(2)}, u32[]{:S(2)}) collective-permute-start(bf16[256,256]{1,0:T(8,128)(2,1)S(1)} %copy-done.7), channel_id=1, source_target_pairs={{0,1},{1,0},{2,3},{3,2},{4,5},{5,4},{6,7},{7,6},{8,9},{9,8},{10,11... | collective-permute-start | bytes 393224 | tf_op jit(solution)/shard_map/ppermute | solution.py:67
  17.2 16.1 %copy-start = (bf16[256,7168]{1,0:T(8,128)(2,1)}, bf16[256,7168]{1,0:T(8,128)(2,1)S(1)}, u32[]{:S(2)}) copy-start(bf16[256,7168]{1,0:T(8,128)(2,1)S(1)} %deal.2.keep) | copy-start | bytes 11010052
  17.2 16.1 %copy-start.3 = (bf16[256,7168]{1,0:T(8,128)(2,1)}, bf16[256,7168]{1,0:T(8,128)(2,1)S(1)}, u32[]{:S(2)}) copy-start(bf16[256,7168]{1,0:T(8,128)(2,1)S(1)} %collective-permute-done.1.got) | copy-start | bytes 11010052
  26.6 17.0 %collective-permute-start.4 = (bf16[1792,256]{1,0:T(8,128)(2,1)S(1)}, bf16[1792,256]{1,0:T(8,128)(2,1)S(1)}, u32[]{:S(2)}, u32[]{:S(2)}) collective-permute-start(bf16[1792,256]{1,0:T(8,128)(2,1)S(1)} %get-tuple-element.67), channel_id=1, source_target_pairs={{0,8},{1,3},{2,10},{3,5},{4,12},{5,7},{6,14},{7,1},{8,16},{9,11},{... | collective-permute-start | bytes 2752520 | tf_op jit(solution)/shard_map/ppermute | solution.py:46
  27.9 15.7 %collective-permute-start.5 = (bf16[1792,256]{1,0:T(8,128)(2,1)S(1)}, bf16[1792,256]{1,0:T(8,128)(2,1)S(1)}, u32[]{:S(2)}, u32[]{:S(2)}) collective-permute-start(bf16[1792,256]{1,0:T(8,128)(2,1)S(1)} %get-tuple-element.68), channel_id=1, source_target_pairs={{0,24},{1,7},{2,26},{3,1},{4,28},{5,3},{6,30},{7,5},{8,0},{9,15},{... | collective-permute-start | bytes 2752520 | tf_op jit(solution)/shard_map/ppermute | solution.py:46
  29.4 11.5 %collective-permute-start.6 = (bf16[896,256]{1,0:T(8,128)(2,1)S(1)}, bf16[896,256]{1,0:T(8,128)(2,1)S(1)}, u32[]{:S(2)}, u32[]{:S(2)}) collective-permute-start(bf16[896,256]{1,0:T(8,128)(2,1)S(1)} %collective-permute-done.2.rest_1_), channel_id=1, source_target_pairs={{0,32},{32,64},{64,96},{96,128},{128,160},{160,192},{192,224},{224... | collective-permute-start | bytes 1376264 | tf_op jit(solution)/shard_map/ppermute | solution.py:59
  29.4 11.5 %collective-permute-start.7 = (bf16[896,256]{1,0:T(8,128)(2,1)S(1)}, bf16[896,256]{1,0:T(8,128)(2,1)S(1)}, u32[]{:S(2)}, u32[]{:S(2)}) collective-permute-start(bf16[896,256]{1,0:T(8,128)(2,1)S(1)} %collective-permute-done.3.rest_2_), channel_id=1, source_target_pairs={{0,224},{32,0},{64,32},{96,64},{128,96},{160,128},{192,160},{224,1... | collective-permute-start | bytes 1376264 | tf_op jit(solution)/shard_map/ppermute | solution.py:59
  40.9 12.5 %collective-permute-start.10 = (bf16[896,256]{1,0:T(8,128)(2,1)S(1)}, bf16[896,256]{1,0:T(8,128)(2,1)S(1)}, u32[]{:S(2)}, u32[]{:S(2)}) collective-permute-start(bf16[896,256]{1,0:T(8,128)(2,1)S(1)} %collective-permute-done.6.rest_0_), channel_id=1, source_target_pairs={{0,32},{32,64},{64,96},{96,128},{128,160},{160,192},{192,224},{224... | collective-permute-start | bytes 1376264 | tf_op jit(solution)/shard_map/ppermute | solution.py:59
  40.9 12.5 %collective-permute-start.11 = (bf16[896,256]{1,0:T(8,128)(2,1)S(1)}, bf16[896,256]{1,0:T(8,128)(2,1)S(1)}, u32[]{:S(2)}, u32[]{:S(2)}) collective-permute-start(bf16[896,256]{1,0:T(8,128)(2,1)S(1)} %collective-permute-done.7.rest_1_), channel_id=1, source_target_pairs={{0,224},{32,0},{64,32},{96,64},{128,96},{160,128},{192,160},{224,1... | collective-permute-start | bytes 1376264 | tf_op jit(solution)/shard_map/ppermute | solution.py:59
  43.6 1.8 %copy-start.11 = (bf16[1792,256]{1,0:T(8,128)(2,1)}, bf16[1792,256]{1,0:T(8,128)(2,1)S(1)}, u32[]{:S(2)}) copy-start(bf16[1792,256]{1,0:T(8,128)(2,1)S(1)} %collective-permute-done.4) | copy-start | bytes 2752516
  44.6 9.2 %collective-permute-start.8 = (bf16[896,256]{1,0:T(8,128)(2,1)}, bf16[896,256]{1,0:T(8,128)(2,1)}, u32[]{:S(2)}, u32[]{:S(2)}) collective-permute-start(bf16[896,256]{1,0:T(8,128)(2,1)} %slice_add_fusion.1), channel_id=1, source_target_pairs={{0,8},{1,3},{2,10},{3,5},{4,12},{5,7},{6,14},{7,1},{8,16},{9,11},{... | collective-permute-start | bytes 1376264 | tf_op jit(solution)/shard_map/ppermute | solution.py:46
  45.4 8.4 %collective-permute-start.9 = (bf16[896,256]{1,0:T(8,128)(2,1)}, bf16[896,256]{1,0:T(8,128)(2,1)}, u32[]{:S(2)}, u32[]{:S(2)}) collective-permute-start(bf16[896,256]{1,0:T(8,128)(2,1)} %slice_add_fusion), channel_id=1, source_target_pairs={{0,24},{1,7},{2,26},{3,1},{4,28},{5,3},{6,30},{7,5},{8,0},{9,15},{... | collective-permute-start | bytes 1376264 | tf_op jit(solution)/shard_map/ppermute | solution.py:46
  48.1 2.0 %copy-start.1 = (bf16[256,7168]{1,0:T(8,128)(2,1)S(1)}, bf16[256,7168]{1,0:T(8,128)(2,1)}, u32[]{:S(2)}) copy-start(bf16[256,7168]{1,0:T(8,128)(2,1)} %copy-done) | copy-start | bytes 11010052
  50.1 2.0 %copy-start.4 = (bf16[256,7168]{1,0:T(8,128)(2,1)S(1)}, bf16[256,7168]{1,0:T(8,128)(2,1)}, u32[]{:S(2)}) copy-start(bf16[256,7168]{1,0:T(8,128)(2,1)} %copy-done.3) | copy-start | bytes 11010052
  53.5 12.3 %collective-permute-start.15 = (bf16[512,256]{1,0:T(8,128)(2,1)S(1)}, bf16[512,256]{1,0:T(8,128)(2,1)S(1)}, u32[]{:S(2)}, u32[]{:S(2)}) collective-permute-start(bf16[512,256]{1,0:T(8,128)(2,1)S(1)} %slice.30), channel_id=1, source_target_pairs={{0,32},{32,64},{64,96},{96,128},{128,160},{160,192},{192,224},{224... | collective-permute-start | bytes 786440 | tf_op jit(solution)/shard_map/ppermute | solution.py:59
  53.8 9.3 %copy-start.2 = (bf16[256,7168]{1,0:T(8,128)(2,1)S(1)}, bf16[256,7168]{1,0:T(8,128)(2,1)}, u32[]{:S(2)}) copy-start(bf16[256,7168]{1,0:T(8,128)(2,1)} %copy-done) | copy-start | bytes 11010052
  53.8 9.3 %copy-start.5 = (bf16[256,7168]{1,0:T(8,128)(2,1)S(1)}, bf16[256,7168]{1,0:T(8,128)(2,1)}, u32[]{:S(2)}) copy-start(bf16[256,7168]{1,0:T(8,128)(2,1)} %copy-done.3) | copy-start | bytes 11010052
  55.7 10.1 %collective-permute-start.14 = (bf16[448,256]{1,0:T(8,128)(2,1)S(1)}, bf16[448,256]{1,0:T(8,128)(2,1)S(1)}, u32[]{:S(2)}, u32[]{:S(2)}) collective-permute-start(bf16[448,256]{1,0:T(8,128)(2,1)S(1)} %get-tuple-element.111), channel_id=1, source_target_pairs={{0,6},{1,25},{2,0},{3,27},{4,2},{5,29},{6,4},{7,31},{8,14},{9,1},{... | collective-permute-start | bytes 688136 | tf_op jit(solution)/shard_map/ppermute | solution.py:55
  59.5 6.5 %collective-permute-start.13 = (bf16[448,256]{1,0:T(8,128)(2,1)S(1)}, bf16[448,256]{1,0:T(8,128)(2,1)S(1)}, u32[]{:S(2)}, u32[]{:S(2)}) collective-permute-start(bf16[448,256]{1,0:T(8,128)(2,1)S(1)} %get-tuple-element.112), channel_id=1, source_target_pairs={{0,4},{1,17},{2,6},{3,19},{4,0},{5,21},{6,2},{7,23},{8,12},{9,25},... | collective-permute-start | bytes 688136 | tf_op jit(solution)/shard_map/ppermute | solution.py:55
  60.0 8.6 %collective-permute-start.12 = (bf16[448,256]{1,0:T(8,128)(2,1)S(1)}, bf16[448,256]{1,0:T(8,128)(2,1)S(1)}, u32[]{:S(2)}, u32[]{:S(2)}) collective-permute-start(bf16[448,256]{1,0:T(8,128)(2,1)S(1)} %get-tuple-element.113), channel_id=1, source_target_pairs={{0,2},{1,9},{2,4},{3,11},{4,6},{5,13},{6,0},{7,15},{8,10},{9,17},{... | collective-permute-start | bytes 688136 | tf_op jit(solution)/shard_map/ppermute | solution.py:55
  60.7 5.1 %collective-permute-start.16 = (bf16[384,256]{1,0:T(8,128)(2,1)S(1)}, bf16[384,256]{1,0:T(8,128)(2,1)S(1)}, u32[]{:S(2)}, u32[]{:S(2)}) collective-permute-start(bf16[384,256]{1,0:T(8,128)(2,1)S(1)} %slice.31), channel_id=1, source_target_pairs={{0,224},{32,0},{64,32},{96,64},{128,96},{160,128},{192,160},{224,1... | collective-permute-start | bytes 589832 | tf_op jit(solution)/shard_map/ppermute | solution.py:59
  69.6 50.2 %copy-start.8 = (bf16[1792,256]{1,0:T(8,128)(2,1)S(1)}, bf16[1792,256]{1,0:T(8,128)(2,1)}, u32[]{:S(2)}) copy-start(bf16[1792,256]{1,0:T(8,128)(2,1)} %right.1) | copy-start | bytes 2752516
  69.6 50.2 %copy-start.9 = (f32[256,256]{1,0:T(8,128)S(1)}, f32[256,256]{1,0:T(8,128)}, u32[]{:S(2)}) copy-start(f32[256,256]{1,0:T(8,128)} %left_stat.1) | copy-start | bytes 786436
  69.7 50.2 %copy-start.10 = (f32[256,256]{1,0:T(8,128)S(1)}, f32[256,256]{1,0:T(8,128)}, u32[]{:S(2)}) copy-start(f32[256,256]{1,0:T(8,128)} %right_stat.1) | copy-start | bytes 786436
  69.7 5.1 %collective-permute-start.17 = (f32[256,256]{1,0:T(8,128)S(1)}, f32[256,256]{1,0:T(8,128)S(1)}, u32[]{:S(2)}, u32[]{:S(2)}) collective-permute-start(f32[256,256]{1,0:T(8,128)S(1)} %get-tuple-element.104), channel_id=1, source_target_pairs={{0,1},{1,0},{2,3},{3,2},{4,5},{5,4},{6,7},{7,6},{8,9},{9,8},{10,11... | collective-permute-start | bytes 786440 | tf_op jit(solution)/shard_map/ppermute | solution.py:67
  75.8 1.8 %collective-permute-start.18 = (f32[128,768]{1,0:T(8,128)S(1)}, f32[128,768]{1,0:T(8,128)S(1)}, u32[]{:S(2)}, u32[]{:S(2)}) collective-permute-start(f32[128,768]{1,0:T(8,128)S(1)} %get-tuple-element.110), channel_id=1, source_target_pairs={{0,1},{1,0},{2,3},{3,2},{4,5},{5,4},{6,7},{7,6},{8,9},{9,8},{10,11... | collective-permute-start | bytes 1179656 | tf_op jit(solution)/shard_map/ppermute | solution.py:67
  114.3 5.6 %collective-permute-start.19 = (f32[128,768]{1,0:T(8,128)S(1)}, f32[128,768]{1,0:T(8,128)S(1)}, u32[]{:S(2)}, u32[]{:S(2)}) collective-permute-start(f32[128,768]{1,0:T(8,128)S(1)} %bitcast.23), channel_id=1, source_target_pairs={{0,1},{1,0},{2,3},{3,2},{4,5},{5,4},{6,7},{7,6},{8,9},{9,8},{10,11... | collective-permute-start | bytes 1179656 | tf_op jit(solution)/shard_map/ppermute | solution.py:67
  (3 other events, 5.2 us)
